TPU v7x, 512 devices: a whole 4x4x16 slice. The times are simulated.
512 devices in a mesh: dp: 16 (over x_hi, y, core), expert: 32 (over x_lo, z).
Axes of the slice: x: 4 (x_hi: 2, x_lo: 2; x = x_hi * 2 + x_lo), y: 4, z: 16, core: 2. Of those that a mesh axis runs over, the one named last changes fastest.
Arguments:
- tokens: bfloat16 [65536, 1024], P(('dp', 'expert')), may hold values from -6 to 6
- cotangent: bfloat16 [65536, 1024], P(('dp', 'expert')), may hold values from -6 to 6
- picks: int32 [512, 64], P(('dp', 'expert')), may hold values from 0 to 127
- gates: float32 [512, 64], P(('dp', 'expert')), may hold values from 0.1 to 1
- w_gate: bfloat16 [64, 2816, 1024], P('expert', 'dp'), may hold values from -0.1875 to 0.1875
- w_up: bfloat16 [64, 2816, 1024], P('expert', 'dp'), may hold values from -0.1875 to 0.1875
- w_down: bfloat16 [64, 2816, 1024], P('expert', 'dp'), may hold values from -0.109375 to 0.109375
Outputs:
- grad_tokens: bfloat16 [65536, 1024], P(('dp', 'expert'))
- grad_gate: bfloat16 [64, 2816, 1024], P('expert', 'dp')
- grad_up: bfloat16 [64, 2816, 1024], P('expert', 'dp')
- grad_down: bfloat16 [64, 2816, 1024], P('expert', 'dp')
Inputs may be any that keep to these rules, and one draw needn't show every extreme that they name: picks[s, e] is the row, among the 128 tokens of device s, that expert e takes from device s.
All inputs are finite; a program needn't handle non-finite values.
Results may differ from a plain program's by a relative error of at most 0.02.
Values may be sent and summed in bfloat16 or wider, within the bound.
No kernel may reach another device: no remote copies, remote signals or barrier semaphores. Data moves between devices by JAX's collectives and lax.ppermute only.
A program may use at most 64 MiB of HBM per device.

v0:
```python
import jax
import jax.numpy as jnp
from jax import lax
from jax.sharding import PartitionSpec as P


def shards(tokens, cotangent, picks, gates, w_gate, w_up, w_down):
    expert_count = lax.axis_size("expert")
    token_rows, width = tokens.shape
    local_experts = w_gate.shape[0]
    chosen_row = picks[0]
    selector = (chosen_row[:, None] == jnp.arange(token_rows, dtype=jnp.int32)[None, :]).astype(
        jnp.bfloat16
    )
    chosen = jnp.dot(selector, tokens, preferred_element_type=jnp.float32).astype(jnp.bfloat16)
    picked_grad = jnp.dot(selector, cotangent, preferred_element_type=jnp.float32)
    scaled = (picked_grad * gates[0][:, None]).astype(jnp.bfloat16)
    layout = (expert_count, local_experts, width)
    got_x, got_dy = (
        lax.all_to_all(chosen.reshape(layout), "expert", split_axis=0, concat_axis=0, tiled=True),
        lax.all_to_all(scaled.reshape(layout), "expert", split_axis=0, concat_axis=0, tiled=True),
    )
    all_x, all_dy = (
        lax.all_gather(got_x, "dp", axis=0, tiled=True),
        lax.all_gather(got_dy, "dp", axis=0, tiled=True),
    )
    pre_gate = jnp.einsum("sed,efd->esf", all_x, w_gate, preferred_element_type=jnp.float32)
    pre_up = jnp.einsum("sed,efd->esf", all_x, w_up, preferred_element_type=jnp.float32)
    sigmoid_g = jax.nn.sigmoid(pre_gate)
    active = pre_gate * sigmoid_g
    hidden = (active * pre_up).astype(jnp.bfloat16)
    grad_hidden = jnp.einsum("sed,efd->esf", all_dy, w_down, preferred_element_type=jnp.float32)
    grad_down = jnp.einsum(
        "esf,sed->efd", hidden, all_dy, preferred_element_type=jnp.float32
    ).astype(jnp.bfloat16)
    d_up = (grad_hidden * active).astype(jnp.bfloat16)
    d_gate = (grad_hidden * pre_up * sigmoid_g * (1.0 + pre_gate * (1.0 - sigmoid_g))).astype(
        jnp.bfloat16
    )
    grad_gate = jnp.einsum(
        "esf,sed->efd", d_gate, all_x, preferred_element_type=jnp.float32
    ).astype(jnp.bfloat16)
    grad_up = jnp.einsum("esf,sed->efd", d_up, all_x, preferred_element_type=jnp.float32).astype(
        jnp.bfloat16
    )
    first = jnp.einsum("esf,efd->sed", d_gate, w_gate, preferred_element_type=jnp.float32)
    second = jnp.einsum("esf,efd->sed", d_up, w_up, preferred_element_type=jnp.float32)
    summed = lax.psum_scatter(
        (first + second).astype(jnp.bfloat16), "dp", scatter_dimension=0, tiled=True
    ).astype(jnp.float32)
    returned = lax.all_to_all(
        summed.astype(jnp.bfloat16), "expert", split_axis=0, concat_axis=0, tiled=True
    ).astype(summed.dtype)
    back_rows = returned.reshape(expert_count * local_experts, width)
    grad_tokens = jax.ops.segment_sum(back_rows, chosen_row, num_segments=token_rows).astype(
        jnp.bfloat16
    )
    return (grad_tokens, grad_gate, grad_up, grad_down)


def solution(mesh):
    return jax.shard_map(
        shards,
        mesh=mesh,
        in_specs=(
            P(("dp", "expert"), None),
            P(("dp", "expert"), None),
            P(("dp", "expert"), None),
            P(("dp", "expert"), None),
            P("expert", "dp", None),
            P("expert", "dp", None),
            P("expert", "dp", None),
        ),
        out_specs=(
            P(("dp", "expert"), None),
            P("expert", "dp", None),
            P("expert", "dp", None),
            P("expert", "dp", None),
        ),
        check_vma=False,
    )
```

profile of v0, /device:TPU:1, one launch (start us, length us, event | category | flops | bytes accessed | tf_op | source)
XLA Modules:
  0.0 298.3 jit_solution(9503811767197228681)
XLA Ops:
  7.2 0.0 copy-start
  7.2 0.0 all-gather.5.cloned.1.call-start
  7.2 1.2 convolution_convert_fusion.3
  8.5 0.1 reshape.23
  8.5 31.3 %all_to_all.15 = bf16[32,2,1024]{2,1,0:T(2,128)(2,1)S(1)} all-to-all(bf16[32,2,1024]{2,1,0:T(2,128)(2,1)S(1)} %reshape.23), channel_id=1, replica_groups=mesh['dp'=16,'expert'=32] {'expert'}, dimensions={0} | all-to-all | bytes 262144 | tf_op jit(solution)/shard_map/all_to_all | solution.py:20
  39.9 0.7 copy.17
  40.6 0.0 all-gather.5.cloned.1.call-update
  40.6 0.0 all-gather.3.cloned.1.call-start
  40.6 1.2 fusion.1
  41.8 0.1 reshape.22
  41.9 0.0 copy-start.2
  41.9 19.1 %all_to_all.16 = bf16[32,2,1024]{2,1,0:T(2,128)(2,1)S(1)} all-to-all(bf16[32,2,1024]{2,1,0:T(2,128)(2,1)S(1)} %reshape.22), channel_id=1, replica_groups=mesh['dp'=16,'expert'=32] {'expert'}, dimensions={0} | all-to-all | bytes 262144 | tf_op jit(solution)/shard_map/all_to_all | solution.py:21
  61.0 0.7 copy.16
  61.7 0.0 all-gather.3.cloned.1.call-update
  61.7 0.0 reduce-scatter.2.cloned.1.call-start
  61.7 36.2 %all-gather.5.cloned.1.call-done = bf16[512,2,1024]{2,0,1:T(8,128)(2,1)} async-done(((bf16[32,2,1024]{2,0,1:T(8,128)(2,1)}), bf16[512,2,1024]{2,0,1:T(8,128)(2,1)}) %all-gather.5.cloned.1.call-update) | async-done | bytes 2097168 | tf_op jit(solution)/shard_map/all_gather | solution.py:24
  98.0 0.0 copy-done
  98.0 0.0 copy-start.1
  98.0 3.5 %fusion.10 = f32[2,512,176]{1,2,0:T(8,128)} fusion(bf16[512,2,1024]{2,0,1:T(8,128)(2,1)} %all-gather.5.cloned.1.call-done, bf16[2,176,1024]{2,1,0:T(8,128)(2,1)S(1)} %copy-done), kind=kOutput, calls=%fused_computation.21 | convolution fusion | flops 369098752 | bytes 3538944 | tf_op jit(solution)/shard_map/sed,efd->esf/dot_general | solution.py:27
  101.4 0.0 copy-done.2
  101.4 0.0 copy-done.1
  101.4 1.7 fusion.9
  103.2 60.6 %all-gather.3.cloned.1.call-done = bf16[512,2,1024]{2,0,1:T(8,128)(2,1)} async-done(((bf16[32,2,1024]{2,0,1:T(8,128)(2,1)}), bf16[512,2,1024]{2,0,1:T(8,128)(2,1)}) %all-gather.3.cloned.1.call-update) | async-done | bytes 2097168 | tf_op jit(solution)/shard_map/all_gather | solution.py:25
  163.8 3.1 %multiply_convert_fusion.1 = (bf16[2,512,176]{1,2,0:T(8,128)(2,1)S(1)}, bf16[2,512,176]{1,2,0:T(8,128)(2,1)S(1)}) fusion(f32[2,512,176]{1,2,0:T(8,128)} %fusion.10, f32[2,512,176]{1,2,0:T(8,128)} %fusion.9, bf16[512,2,1024]{2,0,1:T(8,128)(2,1)} %all-gather.3.cloned.1.call-done, bf16[2,176,1024]{2,1,0:T(8,128)(2,1)} %param.13), kind=kOutput, calls=%fused_computation.10 | convolution fusion | flops 371441664 | bytes 4980736 | tf_op jit(solution)/shard_map/sed,efd->esf/dot_general | solution.py:32
  166.9 0.0 copy-start.5
  166.9 0.0 copy-start.3
  166.9 0.8 fusion.11
  167.7 0.0 copy-done.5
  167.7 0.1 copy-done.3
  167.8 2.1 fusion
  169.9 0.0 copy-start.4
  169.9 0.0 reduce-scatter.2.cloned.1.call-update
  169.9 1.0 copy-done.4
  170.9 0.0 copy-start.6
  170.9 1.4 convolution_convert_fusion.1
  172.3 88.5 %reduce-scatter.2.cloned.1.call-done = bf16[32,2,1024]{2,0,1:T(8,128)(2,1)} async-done(((bf16[512,2,1024]{2,0,1:T(8,128)(2,1)}), bf16[32,2,1024]{2,0,1:T(8,128)(2,1)}) %reduce-scatter.2.cloned.1.call-update) | async-done | bytes 131088 | tf_op jit(solution)/shard_map/reduce_scatter | solution.py:48
  260.8 1.7 copy.18
  262.5 12.7 %all-to-all-start.2 = ((bf16[32,2,1024]{2,1,0:T(2,128)(2,1)}), bf16[32,2,1024]{2,1,0:T(2,128)(2,1)S(1)}, u32[]{:S(2)}, u32[]{:S(2)}) async-start(bf16[32,2,1024]{2,1,0:T(2,128)(2,1)} %copy.18), calls=%async_computation.3 | async-start | bytes 262144 | tf_op jit(solution)/shard_map/all_to_all | solution.py:51
  275.2 0.0 copy-done.6
  275.2 0.0 copy-start.7
  275.2 0.0 copy-start.8
  275.2 1.4 convolution_convert_fusion.2
  276.7 0.0 copy-done.7
  276.7 0.0 copy-done.8
  276.7 3.1 %convolution_convert_fusion = bf16[2,176,1024]{2,1,0:T(8,128)(2,1)} fusion(bf16[512,2,1024]{2,0,1:T(8,128)(2,1)} %all-gather.3.cloned.1.call-done, f32[2,512,176]{1,2,0:T(8,128)S(1)} %copy-done.8, f32[2,512,176]{1,2,0:T(8,128)S(1)} %copy-done.7), kind=kOutput, calls=%fused_computation.3 | convolution fusion | flops 370540544 | bytes 4259840 | tf_op jit(solution)/shard_map/esf,sed->efd/dot_general | solution.py:33
  279.7 9.9 %all-to-all-done.2 = bf16[32,2,1024]{2,1,0:T(2,128)(2,1)S(1)} async-done(((bf16[32,2,1024]{2,1,0:T(2,128)(2,1)}), bf16[32,2,1024]{2,1,0:T(2,128)(2,1)S(1)}, u32[]{:S(2)}, u32[]{:S(2)}) %all-to-all-start.2) | async-done | bytes 131104 | tf_op jit(solution)/shard_map/all_to_all | solution.py:51
  289.7 1.3 scatter_custom_fusion
  291.0 0.7 convert_element_type.43
  (1 shorter events, 0.0 us)
Async XLA Ops:
  7.2 90.8 %copy-start = (bf16[2,176,1024]{2,1,0:T(8,128)(2,1)S(1)}, bf16[2,176,1024]{2,1,0:T(8,128)(2,1)}, u32[]{:S(2)}) copy-start(bf16[2,176,1024]{2,1,0:T(8,128)(2,1)} %param.11) | copy-start | bytes 2162692
  7.2 90.8 %all-gather.5.cloned.1.call-start = ((), (), s32[]{:S(2)}) async-start(), calls=%async_computation.5 | async-start | bytes 2228224 | tf_op jit(solution)/shard_map/all_gather | solution.py:24
  40.6 123.2 %all-gather.3.cloned.1.call-start = ((), (), s32[]{:S(2)}) async-start(), calls=%async_computation.4 | async-start | bytes 2228224 | tf_op jit(solution)/shard_map/all_gather | solution.py:25
  41.9 59.5 %copy-start.2 = (bf16[2,176,1024]{2,1,0:T(8,128)(2,1)S(1)}, bf16[2,176,1024]{2,1,0:T(8,128)(2,1)}, u32[]{:S(2)}) copy-start(bf16[2,176,1024]{2,1,0:T(8,128)(2,1)} %param.12) | copy-start | bytes 2162692
  61.7 199.1 %reduce-scatter.2.cloned.1.call-start = ((), (), s32[]{:S(2)}) async-start(), calls=%async_computation.6 | async-start | bytes 2228224 | tf_op jit(solution)/shard_map/reduce_scatter | solution.py:48
  98.0 3.5 %copy-start.1 = (bf16[512,2,1024]{2,0,1:T(8,128)(2,1)S(1)}, bf16[512,2,1024]{2,0,1:T(8,128)(2,1)}, u32[]{:S(2)}) copy-start(bf16[512,2,1024]{2,0,1:T(8,128)(2,1)} %all-gather.5.cloned.1.call-done) | copy-start | bytes 6291460
  166.9 0.8 copy-start.5
  166.9 0.8 copy-start.3
  169.9 1.0 copy-start.4
  170.9 104.3 %copy-start.6 = (bf16[2,512,176]{1,2,0:T(8,128)(2,1)S(1)}, bf16[2,512,176]{1,2,0:T(8,128)(2,1)}, u32[]{:S(2)}) copy-start(bf16[2,512,176]{1,2,0:T(8,128)(2,1)} %copy-done.5) | copy-start | bytes 1081348
  262.5 27.2 %all-to-all-start.2 = ((bf16[32,2,1024]{2,1,0:T(2,128)(2,1)}), bf16[32,2,1024]{2,1,0:T(2,128)(2,1)S(1)}, u32[]{:S(2)}, u32[]{:S(2)}) async-start(bf16[32,2,1024]{2,1,0:T(2,128)(2,1)} %copy.18), calls=%async_computation.3 | async-start | bytes 262144 | tf_op jit(solution)/shard_map/all_to_all | solution.py:51
  275.2 1.4 copy-start.7
  275.2 1.4 copy-start.8
Sparse Core Ops, SparseCore 0:
  40.7 57.2 all-gather.4
  101.9 61.7 all-gather.2
  170.1 90.6 reduce-scatter.1
where the time goes:
time: 300 us; the launch traced here: 298 us
  waiting for transfers between devices  195 us (65%)
  blocking collectives  50.4 us (17%)
  matrix products  19.5 us (6%)
  between operations  13.9 us (5%)
  starting transfers between devices  12.9 us (4%)
  local copies, waits for them, and re-layouts  4.26 us (1%)
    reduce_scatter x1, waiting for transfers between devices, shards(): lax.psum_scatter((first + second).astype(jnp.bfloat16), 'dp', scatter_dim...  88.5 us
    all_gather x1, waiting for transfers between devices, shards(): lax.all_gather(got_dy, 'dp', axis=0, tiled=True)  60.6 us
    all_gather x1, waiting for transfers between devices, shards(): lax.all_gather(got_x, 'dp', axis=0, tiled=True)  36.2 us
    all_to_all x1, blocking collectives, shards(): lax.all_to_all(chosen.reshape(layout), 'expert', split_axis=0, concat_axi...  31.3 us
    all_to_all x1, blocking collectives, shards(): lax.all_to_all(scaled.reshape(layout), 'expert', split_axis=0, concat_axi...  19.1 us
    all_to_all x1, starting transfers between devices, shards(): lax.all_to_all(summed.astype(jnp.bfloat16), 'expert', split_axis=0, conca...  12.7 us
    all_to_all x1, waiting for transfers between devices, shards(): lax.all_to_all(summed.astype(jnp.bfloat16), 'expert', split_axis=0, conca...  9.89 us
  transfers between devices with their start and end apart: 4, of which 4 were waited for; matrix products, arithmetic and copies ran while one was open for 4% of the time, Pallas kernels for 0%

commit v1 on v0

v1 whole, which is shorter than its diff:
```python
import jax
import jax.numpy as jnp
from jax import lax
from jax.sharding import Mesh, PartitionSpec as P

AXES = ("xh", "y", "core", "xl", "z")
DEST = ("xl", "z")
BATCH = ("xh", "y")
SWAP = ((0, 1), (1, 0))


def one_hot(rows, count):
    return (rows[:, None] == jnp.arange(count, dtype=jnp.int32)[None, :]).astype(jnp.bfloat16)


def shards(tokens, cotangent, picks, gates, w_gate, w_up, w_down):
    f32, bf16 = jnp.float32, jnp.bfloat16
    token_rows, width = tokens.shape
    groups = lax.axis_size(DEST)
    batches = lax.axis_size(BATCH)
    core = lax.axis_index("core")

    def pair(two):
        return jnp.where(core == 0, two[0], two[1]), jnp.where(core == 0, two[1], two[0])

    own, other = [], []
    for w in (w_gate, w_up, w_down):
        own.append(lax.dynamic_index_in_dim(w, core, 0, keepdims=False))
        other.append(lax.dynamic_index_in_dim(w, 1 - core, 0, keepdims=False))
    got_w = lax.ppermute(jnp.stack(other), "core", SWAP)
    wg, wu, wd = (jnp.concatenate([a, got_w[i]], 0) for i, a in enumerate(own))

    chosen = picks[0].reshape(groups, 2)
    weight = gates[0].reshape(groups, 2)
    keep_row, send_row = pair((chosen[:, 0], chosen[:, 1]))
    keep_gate, send_gate = pair((weight[:, 0], weight[:, 1]))
    order = jnp.concatenate([keep_row, send_row])
    scale = jnp.concatenate([keep_gate, send_gate])
    selector = one_hot(order, token_rows)
    x = jnp.dot(selector, tokens, preferred_element_type=f32).astype(bf16)
    dy = (jnp.dot(selector, cotangent, preferred_element_type=f32) * scale[:, None]).astype(bf16)
    x, dy = x.reshape(2, groups, width), dy.reshape(2, groups, width)
    got = lax.ppermute(jnp.stack([x[1], dy[1]]), "core", SWAP)
    out = jnp.stack([x[0], got[0], dy[0], got[1]], 1)
    rows = lax.all_to_all(out, DEST, split_axis=0, concat_axis=0, tiled=True)
    rows = rows.reshape(groups, 2, 2, width).transpose(1, 0, 2, 3).reshape(2, groups * 2, width)
    everyone = jnp.broadcast_to(rows[None], (batches, 2, groups * 2, width))
    gathered = lax.all_to_all(everyone, BATCH, split_axis=0, concat_axis=0, tiled=True)
    all_x = gathered[:, 0].reshape(-1, width)
    all_dy = gathered[:, 1].reshape(-1, width)

    def nt(a, b):
        return lax.dot_general(a, b, (((1,), (1,)), ((), ())), preferred_element_type=f32)

    def tn(a, b):
        return lax.dot_general(a, b, (((0,), (0,)), ((), ())), preferred_element_type=f32)

    pre_gate = nt(all_x, wg)
    pre_up = nt(all_x, wu)
    grad_hidden = nt(all_dy, wd)
    sig = jax.nn.sigmoid(pre_gate)
    active = pre_gate * sig
    hidden = (active * pre_up).astype(bf16)
    d_up = (grad_hidden * active).astype(bf16)
    d_gate = (grad_hidden * pre_up * sig * (1.0 + pre_gate * (1.0 - sig))).astype(bf16)
    part = (
        jnp.dot(d_gate, wg, preferred_element_type=f32)
        + jnp.dot(d_up, wu, preferred_element_type=f32)
    ).astype(bf16)
    parts = lax.all_to_all(
        part.reshape(batches, groups * 2, width), BATCH, split_axis=0, concat_axis=0, tiled=True
    )
    summed = jnp.sum(parts.astype(f32), 0).astype(bf16)

    grads = jnp.stack([tn(d_gate, all_x), tn(d_up, all_x), tn(hidden, all_dy)]).astype(bf16)
    half = grads.shape[1] // 2
    mine = grads[:, :half]
    theirs = lax.ppermute(grads[:, half:], "core", SWAP)
    first = jnp.where(core == 0, mine, theirs)
    second = jnp.where(core == 0, theirs, mine)
    grads = jnp.stack([first, second], 1)

    back = lax.all_to_all(
        summed.reshape(groups, 2, width), DEST, split_axis=0, concat_axis=0, tiled=True
    )
    away = lax.ppermute(back[:, 1], "core", SWAP)
    returned = jnp.concatenate([back[:, 0], away], 0)
    grad_tokens = lax.dot_general(
        selector, returned, (((0,), (0,)), ((), ())), preferred_element_type=f32
    ).astype(bf16)
    return grad_tokens, grads[0], grads[1], grads[2]


def solution(mesh):
    fine = Mesh(mesh.devices.reshape(2, 4, 2, 2, 16), AXES)
    rows = P(AXES, None)
    weights = P(DEST, ("xh", "y", "core"), None)
    return jax.shard_map(
        shards,
        mesh=fine,
        in_specs=(rows, rows, rows, rows, weights, weights, weights),
        out_specs=(rows, weights, weights, weights),
        check_vma=False,
    )
```

time: 300 us -> 144 us (0.48)
  waiting for transfers between devices: 195 us -> 37.2 us
  starting transfers between devices: 12.9 us -> 39.7 us
  blocking collectives: 50.4 us -> 31 us
  between operations: 13.9 us -> 0.88 us
  other arithmetic: 2.09 us -> 11 us
  local copies, waits for them, and re-layouts: 4.26 us -> 12.6 us
  matrix products: 19.5 us -> 11.2 us
    all_gather x2 -> x0, waiting for transfers between devices: 96.9 us -> none  [the longest x1 60.6 us: shards(): lax.all_gather(got_dy, 'dp', axis=0, tiled=True)]
    reduce_scatter x1 -> x0, waiting for transfers between devices: 88.5 us -> none  [shards(): lax.psum_scatter((first + second).astype(jnp.bfloat16), 'dp', scatter_dim...]
    all_to_all x1 -> x3, waiting for transfers between devices: 9.89 us -> 34 us  [the longest x1 13.2 us: shards(): lax.all_to_all(everyone, BATCH, split_axis=0, concat_axis=0, tiled=True)]
    ppermute x0 -> x4, starting transfers between devices: none -> 22 us  [the longest x1 8.79 us: shards(): got = lax.ppermute(jnp.stack([x[1], dy[1]]), 'core', SWAP)]
    all_to_all x2 -> x1, blocking collectives: 50.4 us -> 31 us  [shards(): rows = lax.all_to_all(out, DEST, split_axis=0, concat_axis=0, tiled=True)]
    dot_general x10 -> x11, matrix products: 19.5 us -> 11.2 us  [the longest x3 4.3 us: tn(): lax.dot_general(a, b, (((0,), (0,)), ((), ())), preferred_element_type=f32)]
    all_to_all x1 -> x3, starting transfers between devices: 12.7 us -> 17.7 us  [the longest x1 6.54 us: shards(): lax.all_to_all(part.reshape(batches, groups * 2, width), BATCH, split_axi...]
    another operation x0 -> x5, other arithmetic: none -> 4.36 us  [the longest x1 2.41 us: shards(): grads = jnp.stack([first, second], 1)]
  transfers between devices with their start and end apart: 4 -> 7, of which waited for: 4 -> 5; matrix products, arithmetic and copies ran while one was open for 4% -> 10% of each run, Pallas kernels for 0% -> 0%
where the time goes in v1:
time: 144 us
  starting transfers between devices  39.7 us (28%)
  waiting for transfers between devices  37.2 us (26%)
  blocking collectives  31 us (22%)
  local copies, waits for them, and re-layouts  12.6 us (9%)
  matrix products  11.2 us (8%)
  other arithmetic  11 us (8%)
    all_to_all x1, blocking collectives, shards(): rows = lax.all_to_all(out, DEST, split_axis=0, concat_axis=0, tiled=True)  31 us
    all_to_all x1, waiting for transfers between devices, shards(): lax.all_to_all(everyone, BATCH, split_axis=0, concat_axis=0, tiled=True)  13.2 us
    all_to_all x1, waiting for transfers between devices, shards(): lax.all_to_all(summed.reshape(groups, 2, width), DEST, split_axis=0, conc...  12 us
    all_to_all x1, waiting for transfers between devices, shards(): lax.all_to_all(part.reshape(batches, groups * 2, width), BATCH, split_axi...  8.79 us
    ppermute x1, starting transfers between devices, shards(): got = lax.ppermute(jnp.stack([x[1], dy[1]]), 'core', SWAP)  8.79 us
    all_to_all x1, starting transfers between devices, shards(): lax.all_to_all(part.reshape(batches, groups * 2, width), BATCH, split_axi...  6.54 us
    all_to_all x1, starting transfers between devices, shards(): lax.all_to_all(everyone, BATCH, split_axis=0, concat_axis=0, tiled=True)  6.36 us
    ppermute x1, starting transfers between devices, shards(): away = lax.ppermute(back[:, 1], 'core', SWAP)  5.65 us
  transfers between devices with their start and end apart: 7, of which 5 were waited for; matrix products, arithmetic and copies ran while one was open for 10% of the time, Pallas kernels for 0%

profile of v1, /device:TPU:1, one launch (start us, length us, event | category | flops | bytes accessed | tf_op | source)
XLA Modules:
  0.0 143.6 jit_solution(18034201994403086476)
XLA Ops:
  0.6 0.0 copy-start
  0.7 0.5 broadcast.29
  1.2 1.3 reduce.16
  2.5 0.1 reshape_squeeze.12
  2.6 0.5 broadcast.28
  3.1 1.3 reduce.15
  4.4 0.1 reshape_squeeze.13
  4.5 0.2 select_reduce_fusion.3
  4.7 0.2 select_reduce_fusion.1
  4.9 0.1 pad_add_fusion
  5.0 0.1 pad_maximum_fusion.11
  5.0 0.0 copy-done
  5.0 0.2 convolution_convert_fusion.4
  5.3 1.2 fusion.3
  6.5 8.8 %collective-permute-start = (bf16[2,32,1024]{2,1,0:T(8,128)(2,1)S(1)}, bf16[2,32,1024]{2,1,0:T(8,128)(2,1)S(1)}, u32[]{:S(2)}, u32[]{:S(2)}) collective-permute-start(bf16[2,32,1024]{2,1,0:T(8,128)(2,1)S(1)} %pad_maximum_fusion.10), channel_id=1, source_target_pairs={{0,32},{32,0},{1,33},{33,1},{2,34},{34,2},{3,35},{35,3},{4,36},{36... | collective-permute-start | bytes 393224 | tf_op jit(solution)/shard_map/ppermute | solution.py:43
  15.3 1.0 collective-permute-done
  16.3 0.2 copy.18
  16.6 31.0 %all_to_all.20 = bf16[32,4,1024]{2,1,0:T(4,128)(2,1)S(1)} all-to-all(bf16[32,4,1024]{2,1,0:T(4,128)(2,1)S(1)} %copy.18), channel_id=1, replica_groups=mesh['xh'=2,'y'=4,'core'=2,'xl'=2,'z'=16] {'xl','z'}, dimensions={0} | all-to-all | bytes 524288 | tf_op jit(solution)/shard_map/all_to_all | solution.py:45
  47.5 0.1 reshape.36
  47.6 0.2 copy.19
  47.9 1.6 %broadcast_in_dim.5 = bf16[8,2,64,1024]{3,2,1,0:T(8,128)(2,1)} broadcast(bf16[2,64,1024]{2,1,0:T(8,128)(2,1)S(1)} %copy.20), dimensions={1,2,3} | broadcast | bytes 2359296 | tf_op jit(solution)/shard_map/broadcast_in_dim | solution.py:47
  49.5 6.4 %all-to-all-start.1 = ((bf16[8,2,64,1024]{3,2,1,0:T(8,128)(2,1)}), bf16[8,2,64,1024]{3,2,1,0:T(8,128)(2,1)S(1)}, u32[]{:S(2)}, u32[]{:S(2)}) async-start(bf16[8,2,64,1024]{3,2,1,0:T(8,128)(2,1)} %broadcast_in_dim.5), calls=%async_computation.1 | async-start | bytes 4194304 | tf_op jit(solution)/shard_map/all_to_all | solution.py:48
  55.9 1.9 %dynamic-slice_bitcast_fusion.2 = (bf16[176,1024]{1,0:T(8,128)(2,1)}, bf16[1,176,1024]{2,1,0:T(8,128)(2,1)S(1)}) fusion(bf16[2,176,1024]{2,1,0:T(8,128)(2,1)} %param.13, s32[]{:T(128)S(6)} %select_n.66, s32[]{:T(128)S(6)} %select_n.67), kind=kLoop, calls=%fused_computation.44 | loop fusion | bytes 1441800 | tf_op jit(solution)/shard_map/jit(dynamic_index_in_dim)/squeeze | solution.py:28
  57.7 1.4 %dynamic-slice_bitcast_fusion = (bf16[176,1024]{1,0:T(8,128)(2,1)S(1)}, bf16[1,176,1024]{2,1,0:T(8,128)(2,1)S(1)}, bf16[1,176,1024]{2,1,0:T(8,128)(2,1)S(1)}, bf16[176,1024]{1,0:T(8,128)(2,1)S(1)}) fusion(bf16[2,176,1024]{2,1,0:T(8,128)(2,1)} %param.11, s32[]{:T(128)S(6)} %select_n.66, s32[]{:T(128)S(6)} %select_n.67, bf16[2,176,1024]{2,1,0:T(8,128)(2,1)} %param.12), kind=kLoop, calls=%fused_computation.42 | loop fusion | bytes 2883592 | tf_op jit(solution)/shard_map/jit(dynamic_index_in_dim)/squeeze | solution.py:28
  59.2 0.1 pad_maximum_fusion.1
  59.3 4.9 %collective-permute-start.1 = (bf16[3,176,1024]{2,1,0:T(8,128)(2,1)S(1)}, bf16[3,176,1024]{2,1,0:T(8,128)(2,1)S(1)}, u32[]{:S(2)}, u32[]{:S(2)}) collective-permute-start(bf16[3,176,1024]{2,1,0:T(8,128)(2,1)S(1)} %pad_maximum_fusion.1), channel_id=1, source_target_pairs={{0,32},{32,0},{1,33},{33,1},{2,34},{34,2},{3,35},{35,3},{4,36},{36... | collective-permute-start | bytes 3244040 | tf_op jit(solution)/shard_map/ppermute | solution.py:30
  64.2 2.3 %collective-permute-done.1 = bf16[3,176,1024]{2,1,0:T(8,128)(2,1)S(1)} collective-permute-done((bf16[3,176,1024]{2,1,0:T(8,128)(2,1)S(1)}, bf16[3,176,1024]{2,1,0:T(8,128)(2,1)S(1)}, u32[]{:S(2)}, u32[]{:S(2)}) %collective-permute-start.1) | collective-permute-done | bytes 1081376 | tf_op jit(solution)/shard_map/ppermute | solution.py:30
  66.5 0.9 slice_bitcast_fusion.1
  67.5 13.2 %all-to-all-done.1 = bf16[8,2,64,1024]{3,2,1,0:T(8,128)(2,1)S(1)} async-done(((bf16[8,2,64,1024]{3,2,1,0:T(8,128)(2,1)}), bf16[8,2,64,1024]{3,2,1,0:T(8,128)(2,1)S(1)}, u32[]{:S(2)}, u32[]{:S(2)}) %all-to-all-start.1) | async-done | bytes 2097184 | tf_op jit(solution)/shard_map/all_to_all | solution.py:48
  80.7 0.0 copy-start.1
  80.7 0.2 fusion.31
  80.8 0.8 copy-done.1
  81.7 0.6 fusion.14
  82.2 0.6 fusion.16
  82.8 0.0 copy-start.2
  82.8 0.0 copy-start.3
  82.8 1.5 %fusion.2 = bf16[1,352,1024]{2,1,0:T(8,128)(2,1)} fusion(bf16[512,1024]{1,0:T(8,128)(2,1)S(1)} %bitcast.69, f32[512,352]{0,1:T(8,128)S(1)} %fusion.16, f32[512,352]{0,1:T(8,128)S(1)} %fusion.14), kind=kOutput, calls=%fused_computation.11 | convolution fusion | flops 370540544 | bytes 3211264 | tf_op jit(solution)/shard_map/dot_general | solution.py:56
  84.3 0.0 copy-done.2
  84.3 0.0 copy-done.3
  84.3 0.8 multiply_convert_fusion.2
  85.1 1.4 fusion.1
  86.5 0.7 fusion.15
  87.3 1.4 fusion
  88.7 1.7 %add_convert_fusion = bf16[512,1024]{1,0:T(8,128)(2,1)} fusion(f32[512,1024]{1,0:T(8,128)S(1)} %fusion.15, bf16[512,352]{0,1:T(8,128)(2,1)S(1)} %get-tuple-element.15, bf16[176,1024]{1,0:T(8,128)(2,1)S(1)} %copy-done.1, bf16[176,1024]{1,0:T(8,128)(2,1)S(1)} %get-tuple-element.22), kind=kOutput, calls=%fused_computation.5 | convolution fusion | flops 371589120 | bytes 4227072 | tf_op jit(solution)/shard_map/dot_general | solution.py:67
  90.4 6.5 %all-to-all-start.2 = ((bf16[8,64,1024]{2,1,0:T(8,128)(2,1)}), bf16[8,64,1024]{2,1,0:T(8,128)(2,1)S(1)}, u32[]{:S(2)}, u32[]{:S(2)}) async-start(bf16[8,64,1024]{2,1,0:T(8,128)(2,1)} %bitcast.16), calls=%async_computation.2 | async-start | bytes 2097152 | tf_op jit(solution)/shard_map/all_to_all | solution.py:70
  97.0 1.8 %pad_maximum_fusion = bf16[3,352,1024]{2,1,0:T(8,128)(2,1)S(1)} fusion(bf16[1,352,1024]{2,1,0:T(8,128)(2,1)} %fusion.2, bf16[1,352,1024]{2,1,0:T(8,128)(2,1)} %fusion.1, bf16[1,352,1024]{2,1,0:T(8,128)(2,1)} %fusion), kind=kLoop, calls=%fused_computation.4 | loop fusion | flops 2162688 | bytes 4325376 | tf_op jit(solution)/shard_map/stack | solution.py:75
  98.8 1.1 slice.116
  99.9 2.7 %collective-permute-start.3 = (bf16[3,176,1024]{2,1,0:T(8,128)(2,1)}, bf16[3,176,1024]{2,1,0:T(8,128)(2,1)}, u32[]{:S(2)}, u32[]{:S(2)}) collective-permute-start(bf16[3,176,1024]{2,1,0:T(8,128)(2,1)} %slice.116), channel_id=1, source_target_pairs={{0,32},{32,0},{1,33},{33,1},{2,34},{34,2},{3,35},{35,3},{4,36},{36... | collective-permute-start | bytes 3244040 | tf_op jit(solution)/shard_map/ppermute | solution.py:78
  102.6 8.8 %all-to-all-done.2 = bf16[8,64,1024]{2,1,0:T(8,128)(2,1)S(1)} async-done(((bf16[8,64,1024]{2,1,0:T(8,128)(2,1)}), bf16[8,64,1024]{2,1,0:T(8,128)(2,1)S(1)}, u32[]{:S(2)}, u32[]{:S(2)}) %all-to-all-start.2) | async-done | bytes 1048608 | tf_op jit(solution)/shard_map/all_to_all | solution.py:70
  111.3 0.8 reduce_sum.12
  112.2 1.6 %reshape.38 = bf16[32,2,1024]{2,1,0:T(2,128)(2,1)} reshape(bf16[64,1024]{1,0:T(8,128)(2,1)} %reduce_sum.12) | data formatting | bytes 262144 | tf_op jit(solution)/shard_map/reshape | solution.py:84
  113.8 4.8 %all-to-all-start.3 = ((bf16[32,2,1024]{2,1,0:T(2,128)(2,1)}), bf16[32,2,1024]{2,1,0:T(2,128)(2,1)}, u32[]{:S(2)}, u32[]{:S(2)}) async-start(bf16[32,2,1024]{2,1,0:T(2,128)(2,1)} %reshape.38), calls=%async_computation.3 | async-start | bytes 262144 | tf_op jit(solution)/shard_map/all_to_all | solution.py:83
  118.6 0.0 collective-permute-done.3
  118.6 2.4 %select_bitcast_fusion = (bf16[3,1,176,1024]{3,2,0,1:T(8,128)(2,1)S(1)}, bf16[3,1,176,1024]{3,2,0,1:T(8,128)(2,1)}) fusion(bf16[3,176,1024]{2,1,0:T(8,128)(2,1)} %collective-permute-done.3, pred[]{:T(512)S(6)} %eq.8, bf16[3,352,1024]{2,1,0:T(8,128)(2,1)S(1)} %pad_maximum_fusion), kind=kLoop, calls=%fused_computation.17 | loop fusion | flops 1081344 | bytes 4325377 | tf_op jit(solution)/shard_map/stack | solution.py:81
  121.0 12.0 %all-to-all-done.3 = bf16[32,2,1024]{2,1,0:T(2,128)(2,1)} async-done(((bf16[32,2,1024]{2,1,0:T(2,128)(2,1)}), bf16[32,2,1024]{2,1,0:T(2,128)(2,1)}, u32[]{:S(2)}, u32[]{:S(2)}) %all-to-all-start.3) | async-done | bytes 131104 | tf_op jit(solution)/shard_map/all_to_all | solution.py:83
  133.0 1.2 fusion.32
  134.2 5.6 %collective-permute-start.2 = (bf16[32,1024]{1,0:T(8,128)(2,1)S(1)}, bf16[32,1024]{1,0:T(8,128)(2,1)S(1)}, u32[]{:S(2)}, u32[]{:S(2)}) collective-permute-start(bf16[32,1024]{1,0:T(8,128)(2,1)S(1)} %bitcast.72), channel_id=1, source_target_pairs={{0,32},{32,0},{1,33},{33,1},{2,34},{34,2},{3,35},{35,3},{4,36},{36... | collective-permute-start | bytes 196616 | tf_op jit(solution)/shard_map/ppermute | solution.py:86
  139.9 2.6 %fusion.8 = (bf16[2,176,1024]{2,1,0:T(8,128)(2,1)}, bf16[2,176,1024]{2,1,0:T(8,128)(2,1)}, bf16[2,176,1024]{2,1,0:T(8,128)(2,1)}) fusion(bf16[3,1,176,1024]{3,2,0,1:T(8,128)(2,1)S(1)} %get-tuple-element.8, bf16[3,1,176,1024]{3,2,0,1:T(8,128)(2,1)} %get-tuple-element.9), kind=kLoop, calls=%fused_computation.24 | loop fusion | flops 1081344 | bytes 4325376 | tf_op jit(solution)/shard_map/squeeze | solution.py:91
  142.5 0.0 collective-permute-done.2
  142.5 1.0 convolution_convert_fusion.3
  (7 shorter events, 0.2 us)
Async XLA Ops:
  0.6 4.4 %copy-start = (bf16[128,1024]{1,0:T(8,128)(2,1)S(1)}, bf16[128,1024]{1,0:T(8,128)(2,1)}, u32[]{:S(2)}) copy-start(bf16[128,1024]{1,0:T(8,128)(2,1)} %param.7) | copy-start | bytes 786436
  6.5 9.8 %collective-permute-start = (bf16[2,32,1024]{2,1,0:T(8,128)(2,1)S(1)}, bf16[2,32,1024]{2,1,0:T(8,128)(2,1)S(1)}, u32[]{:S(2)}, u32[]{:S(2)}) collective-permute-start(bf16[2,32,1024]{2,1,0:T(8,128)(2,1)S(1)} %pad_maximum_fusion.10), channel_id=1, source_target_pairs={{0,32},{32,0},{1,33},{33,1},{2,34},{34,2},{3,35},{35,3},{4,36},{36... | collective-permute-start | bytes 393224 | tf_op jit(solution)/shard_map/ppermute | solution.py:43
  49.5 31.2 %all-to-all-start.1 = ((bf16[8,2,64,1024]{3,2,1,0:T(8,128)(2,1)}), bf16[8,2,64,1024]{3,2,1,0:T(8,128)(2,1)S(1)}, u32[]{:S(2)}, u32[]{:S(2)}) async-start(bf16[8,2,64,1024]{3,2,1,0:T(8,128)(2,1)} %broadcast_in_dim.5), calls=%async_computation.1 | async-start | bytes 4194304 | tf_op jit(solution)/shard_map/all_to_all | solution.py:48
  59.3 7.2 %collective-permute-start.1 = (bf16[3,176,1024]{2,1,0:T(8,128)(2,1)S(1)}, bf16[3,176,1024]{2,1,0:T(8,128)(2,1)S(1)}, u32[]{:S(2)}, u32[]{:S(2)}) collective-permute-start(bf16[3,176,1024]{2,1,0:T(8,128)(2,1)S(1)} %pad_maximum_fusion.1), channel_id=1, source_target_pairs={{0,32},{32,0},{1,33},{33,1},{2,34},{34,2},{3,35},{35,3},{4,36},{36... | collective-permute-start | bytes 3244040 | tf_op jit(solution)/shard_map/ppermute | solution.py:30
  80.7 1.0 copy-start.1
  82.8 1.5 %copy-start.2 = (bf16[176,1024]{1,0:T(8,128)(2,1)S(1)}, bf16[176,1024]{1,0:T(8,128)(2,1)}, u32[]{:S(2)}) copy-start(bf16[176,1024]{1,0:T(8,128)(2,1)} %get-tuple-element.24) | copy-start | bytes 1081348
  82.8 1.5 %copy-start.3 = (bf16[176,1024]{1,0:T(8,128)(2,1)S(1)}, bf16[176,1024]{1,0:T(8,128)(2,1)}, u32[]{:S(2)}) copy-start(bf16[176,1024]{1,0:T(8,128)(2,1)} %get-tuple-element.19) | copy-start | bytes 1081348
  90.4 20.9 %all-to-all-start.2 = ((bf16[8,64,1024]{2,1,0:T(8,128)(2,1)}), bf16[8,64,1024]{2,1,0:T(8,128)(2,1)S(1)}, u32[]{:S(2)}, u32[]{:S(2)}) async-start(bf16[8,64,1024]{2,1,0:T(8,128)(2,1)} %bitcast.16), calls=%async_computation.2 | async-start | bytes 2097152 | tf_op jit(solution)/shard_map/all_to_all | solution.py:70
  99.9 18.7 %collective-permute-start.3 = (bf16[3,176,1024]{2,1,0:T(8,128)(2,1)}, bf16[3,176,1024]{2,1,0:T(8,128)(2,1)}, u32[]{:S(2)}, u32[]{:S(2)}) collective-permute-start(bf16[3,176,1024]{2,1,0:T(8,128)(2,1)} %slice.116), channel_id=1, source_target_pairs={{0,32},{32,0},{1,33},{33,1},{2,34},{34,2},{3,35},{35,3},{4,36},{36... | collective-permute-start | bytes 3244040 | tf_op jit(solution)/shard_map/ppermute | solution.py:78
  113.8 19.2 %all-to-all-start.3 = ((bf16[32,2,1024]{2,1,0:T(2,128)(2,1)}), bf16[32,2,1024]{2,1,0:T(2,128)(2,1)}, u32[]{:S(2)}, u32[]{:S(2)}) async-start(bf16[32,2,1024]{2,1,0:T(2,128)(2,1)} %reshape.38), calls=%async_computation.3 | async-start | bytes 262144 | tf_op jit(solution)/shard_map/all_to_all | solution.py:83
  134.2 8.3 %collective-permute-start.2 = (bf16[32,1024]{1,0:T(8,128)(2,1)S(1)}, bf16[32,1024]{1,0:T(8,128)(2,1)S(1)}, u32[]{:S(2)}, u32[]{:S(2)}) collective-permute-start(bf16[32,1024]{1,0:T(8,128)(2,1)S(1)} %bitcast.72), channel_id=1, source_target_pairs={{0,32},{32,0},{1,33},{33,1},{2,34},{34,2},{3,35},{35,3},{4,36},{36... | collective-permute-start | bytes 196616 | tf_op jit(solution)/shard_map/ppermute | solution.py:86

commit v2 on v1

v2 whole, which is shorter than its diff:
```python
import jax
import jax.numpy as jnp
from jax import lax
from jax.experimental import pallas as pl
from jax.experimental.pallas import tpu as pltpu
from jax.sharding import Mesh, PartitionSpec as P

AXES = ("xh", "y", "core", "xl", "z")
DEST = ("core", "xl", "z")
BATCH = ("xh", "y")
SWAP = ((0, 1), (1, 0))
F32, BF16 = jnp.float32, jnp.bfloat16


def iota(shape, axis):
    return lax.broadcasted_iota(jnp.int32, shape, axis)


def column(row, rows_each):
    count = row.shape[1]
    shape = (count * rows_each, count)
    place = iota(shape, 0) // rows_each
    expert = (place % (count // 2)) * 2 + place // (count // 2)
    spread = jnp.where(iota(shape, 1) == expert, jnp.broadcast_to(row, shape), 0.0)
    return jnp.sum(spread, axis=1, keepdims=True)


def pick_kernel(picks_in, gates_in, tokens_in, cotangent_in, out, picks, gates, both, sems):
    token_rows = tokens_in.shape[0]
    copies = [
        pltpu.make_async_copy(source, target, sems.at[i])
        for i, (source, target) in enumerate(
            (
                (picks_in, picks),
                (gates_in, gates),
                (tokens_in, both.at[pl.ds(0, token_rows)]),
                (cotangent_in, both.at[pl.ds(token_rows, token_rows)]),
            )
        )
    ]
    for copy in copies:
        copy.start()
    copies[0].wait()
    copies[1].wait()
    count = picks.shape[1]
    row = column(picks[...].astype(F32), 2).astype(jnp.int32)
    gate = column(gates[...], 2)
    shape = (2 * count, 2 * token_rows)
    odd = iota((2 * count, 1), 0) % 2
    selector = (iota(shape, 1) == row + odd * token_rows).astype(F32).astype(BF16)
    copies[2].wait()
    copies[3].wait()
    picked = jnp.dot(selector, both[...], preferred_element_type=F32)
    scaled = picked * jnp.where(odd == 1, gate, 1.0)
    out[...] = scaled.reshape(out.shape).astype(BF16)


def spread_kernel(rows, out, both, sems):
    count, width = both.shape[1:]
    for i in range(2):
        half = rows[:, 8 * i : 8 * i + 8, :].astype(F32)
        both[i] = half.reshape(count, width).astype(BF16)
    copies = [
        pltpu.make_async_copy(both, out.at[i], sems.at[i]) for i in range(out.shape[0])
    ]
    for copy in copies:
        copy.start()
    for copy in copies:
        copy.wait()


def sum_kernel(parts, out):
    out[...] = jnp.sum(parts[...].astype(F32), 0).astype(BF16)


def scatter_kernel(picks, returned, out):
    count, token_rows = picks.shape[1], out.shape[0]
    row = column(picks[...].astype(F32), 1).astype(jnp.int32)
    selector = (iota((count, token_rows), 1) == row).astype(F32).astype(BF16)
    out[...] = tn(selector, returned[...]).astype(BF16)


def fill_kernel(core_ref, *refs):
    away = 1 - core_ref[0]
    theirs, outs, sems = refs[:3], refs[6:9], refs[9]
    copies = [
        pltpu.make_async_copy(theirs[i].at[away], outs[i].at[away], sems.at[i]) for i in range(3)
    ]
    for copy in copies:
        copy.start()
    for copy in copies:
        copy.wait()


def nt(a, b):
    return lax.dot_general(a, b, (((1,), (1,)), ((), ())), preferred_element_type=F32)


def tn(a, b):
    return lax.dot_general(a, b, (((0,), (0,)), ((), ())), preferred_element_type=F32)


def products_kernel(got, own, other, down, part, acts):
    batches, _, count, width = got.shape
    x = got[:, 0].reshape(batches * count, width)
    dy = got[:, 1].reshape(batches * count, width)
    for half, gate_up in ((0, own), (1, other)):
        pre_gate = nt(gate_up[0], x)
        pre_up = nt(gate_up[1], x)
        grad_hidden = nt(down[half], dy)
        sig = jax.nn.sigmoid(pre_gate)
        active = pre_gate * sig
        acts[0, half] = (grad_hidden * pre_up * sig * (1.0 + pre_gate * (1.0 - sig))).astype(BF16)
        acts[1, half] = (grad_hidden * active).astype(BF16)
        acts[2, half] = (active * pre_up).astype(BF16)
    total = tn(acts[0, 0], own[0]) + tn(acts[1, 0], own[1])
    total += tn(acts[0, 1], other[0]) + tn(acts[1, 1], other[1])
    part[...] = total.astype(BF16).reshape(part.shape)


def grads_kernel(core_ref, acts, got, gate, up, down, *rest):
    sends, mine, sems = rest[:3], rest[3], rest[4]
    core = core_ref[0]
    rows = got.shape[0] * got.shape[2]
    stores = []
    for i, out in enumerate((gate, up, down)):
        side = got[:, i // 2].reshape(rows, got.shape[3])
        mine[i] = jnp.dot(acts[i, 0], side, preferred_element_type=F32).astype(BF16)
        stores.append(pltpu.make_async_copy(mine.at[i], out.at[core], sems.at[i]))
        stores[-1].start()
        sends[i][...] = jnp.dot(acts[i, 1], side, preferred_element_type=F32).astype(BF16)
    for copy in stores:
        copy.wait()


def shards(tokens, cotangent, picks, gates, w_gate, w_up, w_down):
    token_rows, width = tokens.shape
    count = picks.shape[1]
    units = w_gate.shape[1]
    core = lax.axis_index("core")
    small = pltpu.CompilerParams(vmem_limit_bytes=12 * 2**20)
    full = pltpu.CompilerParams(vmem_limit_bytes=63 * 2**20)
    medium = pltpu.CompilerParams(vmem_limit_bytes=20 * 2**20)
    scalar = pl.BlockSpec(memory_space=pltpu.SMEM)
    near = pl.BlockSpec(memory_space=pltpu.VMEM)
    far = pl.BlockSpec(memory_space=pl.ANY)
    place = core.reshape(1)

    def of(expert, *arrays):
        return jnp.stack(
            [lax.dynamic_index_in_dim(w, expert, 0, keepdims=False) for w in arrays]
        )

    own = of(core, w_gate, w_up)
    other = lax.ppermute(of(1 - core, w_gate, w_up), "core", SWAP)
    down = jnp.concatenate(
        [of(core, w_down), lax.ppermute(of(1 - core, w_down), "core", SWAP)], 0
    )

    out = pl.pallas_call(
        pick_kernel,
        in_specs=[far] * 4,
        out_specs=near,
        out_shape=jax.ShapeDtypeStruct((count, 16, width // 8), BF16),
        scratch_shapes=[
            pltpu.VMEM((1, count), jnp.int32),
            pltpu.VMEM((1, count), F32),
            pltpu.VMEM((2 * token_rows, width), BF16),
            pltpu.SemaphoreType.DMA((4,)),
        ],
        compiler_params=full,
    )(picks, gates, tokens, cotangent)
    rows = lax.all_to_all(out, DEST, split_axis=0, concat_axis=0, tiled=True)
    batches = lax.axis_size(BATCH)
    sources = batches * count
    everyone = pl.pallas_call(
        spread_kernel,
        in_specs=[near],
        out_specs=far,
        out_shape=jax.ShapeDtypeStruct((batches, 2, count, width), BF16),
        scratch_shapes=[
            pltpu.VMEM((2, count, width), BF16),
            pltpu.SemaphoreType.DMA((batches,)),
        ],
        compiler_params=full,
    )(rows)
    got = lax.all_to_all(everyone, BATCH, split_axis=0, concat_axis=0, tiled=True)

    part, acts = pl.pallas_call(
        products_kernel,
        in_specs=[near] * 4,
        out_specs=[near] * 2,
        out_shape=[
            jax.ShapeDtypeStruct((batches, count, width), BF16),
            jax.ShapeDtypeStruct((3, 2, units, sources), BF16),
        ],
        cost_estimate=pl.CostEstimate(
            flops=20 * sources * units * width, bytes_accessed=8 * 2**20, transcendentals=0
        ),
        compiler_params=medium,
    )(got, own, other, down)
    parts = lax.all_to_all(part, BATCH, split_axis=0, concat_axis=0, tiled=True)

    side = jax.ShapeDtypeStruct((units, width), BF16)
    grad = jax.ShapeDtypeStruct((2, units, width), BF16)
    results = pl.pallas_call(
        grads_kernel,
        in_specs=[scalar, near, near],
        out_specs=[far] * 3 + [near] * 3,
        out_shape=[grad] * 3 + [side] * 3,
        scratch_shapes=[pltpu.VMEM((3, units, width), BF16), pltpu.SemaphoreType.DMA((3,))],
        cost_estimate=pl.CostEstimate(
            flops=12 * sources * units * width, bytes_accessed=6 * 2**20, transcendentals=0
        ),
        compiler_params=medium,
    )(place, acts, got)
    theirs = [lax.all_gather(send, "core", axis=0) for send in results[3:]]
    grads = pl.pallas_call(
        fill_kernel,
        in_specs=[scalar] + [near] * 3 + [far] * 3,
        out_specs=[far] * 3,
        out_shape=[grad] * 3,
        input_output_aliases={4: 0, 5: 1, 6: 2},
        scratch_shapes=[pltpu.SemaphoreType.DMA((3,))],
        compiler_params=small,
    )(place, *theirs, *results[:3])
    summed = pl.pallas_call(
        sum_kernel,
        in_specs=[near],
        out_specs=near,
        out_shape=jax.ShapeDtypeStruct((count, width), BF16),
        compiler_params=small,
    )(parts)
    returned = lax.all_to_all(
        summed.reshape(count, 2, width // 2), DEST, split_axis=0, concat_axis=0, tiled=True
    )
    grad_tokens = pl.pallas_call(
        scatter_kernel,
        in_specs=[near, near],
        out_specs=near,
        out_shape=jax.ShapeDtypeStruct((token_rows, width), BF16),
        compiler_params=small,
    )(picks, returned.reshape(count, width))
    return grad_tokens, *grads


def solution(mesh):
    fine = Mesh(mesh.devices.reshape(2, 4, 2, 2, 16), AXES)
    rows = P(AXES, None)
    weights = P(("xl", "z"), ("xh", "y", "core"), None)
    return jax.shard_map(
        shards,
        mesh=fine,
        in_specs=(rows, rows, rows, rows, weights, weights, weights),
        out_specs=(rows, weights, weights, weights),
        check_vma=False,
    )
```

time: 144 us -> 128 us (0.89)
  starting transfers between devices: 39.7 us -> 23.8 us
  blocking collectives: 31 us -> 46.6 us
  Pallas kernels: 0 us -> 12.1 us
  matrix products: 11.2 us -> 0 us
  other arithmetic: 11 us -> 0.21 us
  local copies, waits for them, and re-layouts: 12.6 us -> 7.62 us
    ppermute x4 -> x2, starting transfers between devices: 22 us -> 5.06 us  [the longest x1 3.14 us: shards(): other = lax.ppermute(of(1 - core, w_gate, w_up), 'core', SWAP)]
    pallas_call x0 -> x7, Pallas kernels: none -> 12.1 us  [the longest x1 3.45 us: shards(): pl.pallas_call(products_kernel, in_specs=[near] * 4, out_specs=[near] * 2...]
    dot_general x11 -> x0, matrix products: 11.2 us -> none  [the longest x3 4.3 us: tn(): lax.dot_general(a, b, (((0,), (0,)), ((), ())), preferred_element_type=f32)]
    all_to_all x1, blocking collectives: 31 us -> 39.4 us  [shards(): rows = lax.all_to_all(out, DEST, split_axis=0, concat_axis=0, tiled=True)]
    all_gather x0 -> x3, blocking collectives: none -> 7.15 us  [shards(): theirs = [lax.all_gather(send, 'core', axis=0) for send in results[3:]]]
    all_to_all x1, waiting for transfers between devices: 13.2 us -> 18.1 us  [shards(): lax.all_to_all(everyone, BATCH, split_axis=0, concat_axis=0, tiled=True)]
    unnamed x12 -> x25, local copies, waits for them, and re-layouts: 1.91 us -> 6.69 us
    squeeze x3 -> x0, local copies, waits for them, and re-layouts: 4.24 us -> none  [the longest x2 3.32 us: shards(): own.append(lax.dynamic_index_in_dim(w, core, 0, keepdims=False))]
  transfers between devices with their start and end apart: 7 -> 5, of which waited for: 5 -> 4; matrix products, arithmetic and copies ran while one was open for 10% -> 0% of each run, Pallas kernels for 0% -> 2%
where the time goes in v2:
time: 128 us
  blocking collectives  46.6 us (36%)
  waiting for transfers between devices  36.8 us (29%)
  starting transfers between devices  23.8 us (19%)
  Pallas kernels  12.1 us (9%)
  local copies, waits for them, and re-layouts  7.62 us (6%)
    all_to_all x1, blocking collectives, shards(): rows = lax.all_to_all(out, DEST, split_axis=0, concat_axis=0, tiled=True)  39.4 us
    all_to_all x1, waiting for transfers between devices, shards(): lax.all_to_all(everyone, BATCH, split_axis=0, concat_axis=0, tiled=True)  18.1 us
    all_to_all x1, waiting for transfers between devices, shards(): parts = lax.all_to_all(part, BATCH, split_axis=0, concat_axis=0, tiled=True)  9.78 us
    all_to_all x1, waiting for transfers between devices, shards(): lax.all_to_all(summed.reshape(count, 2, width // 2), DEST, split_axis=0,...  7.27 us
    all_gather x3, blocking collectives, shards(): theirs = [lax.all_gather(send, 'core', axis=0) for send in results[3:]]  7.15 us
    all_to_all x1, starting transfers between devices, shards(): lax.all_to_all(summed.reshape(count, 2, width // 2), DEST, split_axis=0,...  7.04 us
    unnamed x25, local copies, waits for them, and re-layouts  6.69 us
    all_to_all x1, starting transfers between devices, shards(): lax.all_to_all(everyone, BATCH, split_axis=0, concat_axis=0, tiled=True)  6.5 us
  transfers between devices with their start and end apart: 5, of which 4 were waited for; matrix products, arithmetic and copies ran while one was open for 0% of the time, Pallas kernels for 2%

profile of v2, /device:TPU:1, one launch (start us, length us, event | category | flops | bytes accessed | tf_op | source)
XLA Modules:
  0.0 127.9 jit_solution(15783944496770218526)
XLA Ops:
  0.6 2.1 %shard_map.102 = bf16[64,16,128]{2,1,0:T(8,128)(2,1)} custom-call(s32[1,64]{1,0:T(1,128)} %picks.1, f32[1,64]{1,0:T(1,128)} %gates_in.1, bf16[128,1024]{1,0:T(8,128)(2,1)} %tokens_in.1, bf16[128,1024]{1,0:T(8,128)(2,1)} %cotangent_in.1), custom_call_target="tpu_custom_call" | custom-call | tf_op jit(solution)/shard_map/pallas_call | solution.py:160
  2.7 39.4 %all_to_all.20.rows = bf16[64,16,128]{2,1,0:T(8,128)(2,1)} all-to-all(bf16[64,16,128]{2,1,0:T(8,128)(2,1)} %shard_map.102), channel_id=1, replica_groups=mesh['xh'=2,'y'=4,'core'=2,'xl'=2,'z'=16] {'core','xl','z'}, dimensions={0} | all-to-all | bytes 524288 | tf_op jit(solution)/shard_map/all_to_all | solution.py:173
  42.2 2.5 %shard_map.103 = bf16[8,2,64,1024]{3,2,1,0:T(8,128)(2,1)} custom-call(bf16[64,16,128]{2,1,0:T(8,128)(2,1)} %all_to_all.20.rows), custom_call_target="tpu_custom_call" | custom-call | tf_op jit(solution)/shard_map/pallas_call | solution.py:176
  44.7 0.0 copy-start.10
  44.7 0.0 copy-start.11
  44.7 6.5 %all-to-all-start.1 = ((bf16[8,2,64,1024]{3,2,1,0:T(8,128)(2,1)}), bf16[8,2,64,1024]{3,2,1,0:T(8,128)(2,1)S(1)}, u32[]{:S(2)}, u32[]{:S(2)}) async-start(bf16[8,2,64,1024]{3,2,1,0:T(8,128)(2,1)} %shard_map.103), calls=%async_computation.1 | async-start | bytes 4194304 | tf_op jit(solution)/shard_map/all_to_all | solution.py:187
  51.2 0.0 copy-done.10
  51.2 0.0 copy-done.11
  51.2 0.0 copy-start.9
  51.2 0.1 constant_dynamic-slice_fusion.2
  51.4 0.1 pad_maximum_fusion.1
  51.4 3.1 %collective-permute-start = (bf16[2,176,1024]{2,1,0:T(8,128)(2,1)S(1)}, bf16[2,176,1024]{2,1,0:T(8,128)(2,1)S(1)}, u32[]{:S(2)}, u32[]{:S(2)}) collective-permute-start(bf16[2,176,1024]{2,1,0:T(8,128)(2,1)S(1)} %pad_maximum_fusion.1), channel_id=1, source_target_pairs={{0,32},{32,0},{1,33},{33,1},{2,34},{34,2},{3,35},{35,3},{4,36},{36... | collective-permute-start | bytes 2162696 | tf_op jit(solution)/shard_map/ppermute | solution.py:155
  54.6 0.0 copy-done.9
  54.6 0.1 constant_dynamic-slice_fusion.1
  54.7 1.9 %collective-permute-start.1 = (bf16[1,176,1024]{2,1,0:T(8,128)(2,1)S(1)}, bf16[1,176,1024]{2,1,0:T(8,128)(2,1)S(1)}, u32[]{:S(2)}, u32[]{:S(2)}) collective-permute-start(bf16[1,176,1024]{2,1,0:T(8,128)(2,1)S(1)} %get-tuple-element.27), channel_id=1, source_target_pairs={{0,32},{32,0},{1,33},{33,1},{2,34},{34,2},{3,35},{35,3},{4,36},{36... | collective-permute-start | bytes 1081352 | tf_op jit(solution)/shard_map/ppermute | solution.py:157
  56.6 0.1 pad_maximum_fusion.own
  56.7 1.6 %collective-permute-done.1 = bf16[1,176,1024]{2,1,0:T(8,128)(2,1)S(1)} collective-permute-done((bf16[1,176,1024]{2,1,0:T(8,128)(2,1)S(1)}, bf16[1,176,1024]{2,1,0:T(8,128)(2,1)S(1)}, u32[]{:S(2)}, u32[]{:S(2)}) %collective-permute-start.1) | collective-permute-done | bytes 360480 | tf_op jit(solution)/shard_map/ppermute | solution.py:157
  58.2 0.1 pad_maximum_fusion.2.down
  58.3 0.0 collective-permute-done.other
  58.3 0.0 copy-start.5
  58.3 0.8 copy-done.5
  59.2 18.1 %all-to-all-done.1.got = bf16[8,2,64,1024]{3,2,1,0:T(8,128)(2,1)S(1)} async-done(((bf16[8,2,64,1024]{3,2,1,0:T(8,128)(2,1)}), bf16[8,2,64,1024]{3,2,1,0:T(8,128)(2,1)S(1)}, u32[]{:S(2)}, u32[]{:S(2)}) %all-to-all-start.1) | async-done | bytes 2097184 | tf_op jit(solution)/shard_map/all_to_all | solution.py:187
  77.3 0.0 copy-start.6
  77.3 1.1 copy-done.6
  78.4 3.4 %shard_map.104 = (bf16[8,64,1024]{2,1,0:T(8,128)(2,1)S(1)}, bf16[3,2,176,512]{3,2,1,0:T(8,128)(2,1)S(1)}) custom-call(bf16[8,2,64,1024]{3,2,1,0:T(8,128)(2,1)S(1)} %all-to-all-done.1.got, bf16[2,176,1024]{2,1,0:T(8,128)(2,1)S(1)} %pad_maximum_fusion.own, bf16[2,176,1024]{2,1,0:T(8,128)(2,1)S(1)} %copy-done.6, bf16[2,176,1024]{2,1,0:T(8,128)(2,1)S(1)} %pad_maximum_fusion.2.down), custom_call_target="tpu_custom_call" | custom-call | flops 1845493760 | bytes 8388608 | tf_op jit(solution)/shard_map/pallas_call | solution.py:189
  81.9 0.0 copy-start
  81.9 1.0 copy-done
  82.8 0.0 copy-start.7
  82.8 1.0 copy-done.7
  83.9 5.2 %all-to-all-start.2 = ((bf16[8,64,1024]{2,1,0:T(8,128)(2,1)}), bf16[8,64,1024]{2,1,0:T(8,128)(2,1)S(1)}, u32[]{:S(2)}, u32[]{:S(2)}) async-start(bf16[8,64,1024]{2,1,0:T(8,128)(2,1)} %copy-done), calls=%async_computation.2 | async-start | bytes 2097152 | tf_op jit(solution)/shard_map/all_to_all | solution.py:202
  89.1 0.0 copy-start.8
  89.1 1.2 copy-done.8
  90.3 1.9 %shard_map.107 = (bf16[2,176,1024]{2,1,0:T(8,128)(2,1)}, bf16[2,176,1024]{2,1,0:T(8,128)(2,1)}, bf16[2,176,1024]{2,1,0:T(8,128)(2,1)}, bf16[176,1024]{1,0:T(8,12...) custom-call(s32[1]{0:T(128)} %bitcast.core_ref, bf16[3,2,176,512]{3,2,1,0:T(8,128)(2,1)S(1)} %copy-done.8, ...), custom_call_target="tpu_custom_call" | custom-call | flops 1107296256 | bytes 6291456 | tf_op jit(solution)/shard_map/pallas_call | solution.py:206
  92.2 0.0 copy-start.1
  92.2 0.7 copy-done.1
  93.0 0.0 copy-start.3
  93.0 0.7 copy-done.3
  93.7 9.8 %all-to-all-done.2.parts = bf16[8,64,1024]{2,1,0:T(8,128)(2,1)S(1)} async-done(((bf16[8,64,1024]{2,1,0:T(8,128)(2,1)}), bf16[8,64,1024]{2,1,0:T(8,128)(2,1)S(1)}, u32[]{:S(2)}, u32[]{:S(2)}) %all-to-all-start.2) | async-done | bytes 1048608 | tf_op jit(solution)/shard_map/all_to_all | solution.py:202
  103.5 0.0 copy-start.2
  103.5 0.1 shard_map.105
  103.6 0.7 reshape.17
  104.3 7.0 %all-to-all-start.3 = ((bf16[64,2,512]{2,1,0:T(2,128)(2,1)}), bf16[64,2,512]{2,1,0:T(2,128)(2,1)S(1)}, u32[]{:S(2)}, u32[]{:S(2)}) async-start(bf16[64,2,512]{2,1,0:T(2,128)(2,1)} %reshape.17), calls=%async_computation.3 | async-start | bytes 262144 | tf_op jit(solution)/shard_map/all_to_all | solution.py:234
  111.4 2.5 %all-gather = bf16[352,1024]{1,0:T(8,128)(2,1)S(1)} all-gather(bf16[176,1024]{1,0:T(8,128)(2,1)} %copy-done.3), channel_id=2, replica_groups=mesh['xh'=2,'y'=4,'core'=2,'xl'=2,'z'=16] {'core'}, dimensions={0}, use_global_device_ids=true | all-gather | bytes 1081344 | tf_op jit(solution)/shard_map/all_gather | solution.py:217
  113.9 0.0 copy-done.2
  113.9 2.3 %all-gather.1 = bf16[352,1024]{1,0:T(8,128)(2,1)S(1)} all-gather(bf16[176,1024]{1,0:T(8,128)(2,1)S(1)} %copy-done.2), channel_id=3, replica_groups=mesh['xh'=2,'y'=4,'core'=2,'xl'=2,'z'=16] {'core'}, dimensions={0}, use_global_device_ids=true | all-gather | bytes 1081344 | tf_op jit(solution)/shard_map/all_gather | solution.py:217
  116.2 2.3 %all-gather.2 = bf16[352,1024]{1,0:T(8,128)(2,1)S(1)} all-gather(bf16[176,1024]{1,0:T(8,128)(2,1)S(1)} %get-tuple-element.19), channel_id=4, replica_groups=mesh['xh'=2,'y'=4,'core'=2,'xl'=2,'z'=16] {'core'}, dimensions={0}, use_global_device_ids=true | all-gather | bytes 1081344 | tf_op jit(solution)/shard_map/all_gather | solution.py:217
  118.5 0.0 copy-start.4
  118.5 1.0 shard_map.108
  119.5 7.3 %all-to-all-done.3 = bf16[64,2,512]{2,1,0:T(2,128)(2,1)S(1)} async-done(((bf16[64,2,512]{2,1,0:T(2,128)(2,1)}), bf16[64,2,512]{2,1,0:T(2,128)(2,1)S(1)}, u32[]{:S(2)}, u32[]{:S(2)}) %all-to-all-start.3) | async-done | bytes 131104 | tf_op jit(solution)/shard_map/all_to_all | solution.py:234
  126.8 0.0 copy-done.4
  126.8 1.0 shard_map.106
  (1 shorter events, 0.0 us)
Async XLA Ops:
  44.7 6.5 %copy-start.10 = (bf16[2,176,1024]{2,1,0:T(8,128)(2,1)S(1)}, bf16[2,176,1024]{2,1,0:T(8,128)(2,1)}, u32[]{:S(2)}) copy-start(bf16[2,176,1024]{2,1,0:T(8,128)(2,1)} %param.12) | copy-start | bytes 2162692
  44.7 6.5 %copy-start.11 = (bf16[2,176,1024]{2,1,0:T(8,128)(2,1)S(1)}, bf16[2,176,1024]{2,1,0:T(8,128)(2,1)}, u32[]{:S(2)}) copy-start(bf16[2,176,1024]{2,1,0:T(8,128)(2,1)} %param.11) | copy-start | bytes 2162692
  44.7 32.6 %all-to-all-start.1 = ((bf16[8,2,64,1024]{3,2,1,0:T(8,128)(2,1)}), bf16[8,2,64,1024]{3,2,1,0:T(8,128)(2,1)S(1)}, u32[]{:S(2)}, u32[]{:S(2)}) async-start(bf16[8,2,64,1024]{3,2,1,0:T(8,128)(2,1)} %shard_map.103), calls=%async_computation.1 | async-start | bytes 4194304 | tf_op jit(solution)/shard_map/all_to_all | solution.py:187
  51.2 3.4 %copy-start.9 = (bf16[2,176,1024]{2,1,0:T(8,128)(2,1)S(1)}, bf16[2,176,1024]{2,1,0:T(8,128)(2,1)}, u32[]{:S(2)}) copy-start(bf16[2,176,1024]{2,1,0:T(8,128)(2,1)} %param.13) | copy-start | bytes 2162692
  51.4 6.9 %collective-permute-start = (bf16[2,176,1024]{2,1,0:T(8,128)(2,1)S(1)}, bf16[2,176,1024]{2,1,0:T(8,128)(2,1)S(1)}, u32[]{:S(2)}, u32[]{:S(2)}) collective-permute-start(bf16[2,176,1024]{2,1,0:T(8,128)(2,1)S(1)} %pad_maximum_fusion.1), channel_id=1, source_target_pairs={{0,32},{32,0},{1,33},{33,1},{2,34},{34,2},{3,35},{35,3},{4,36},{36... | collective-permute-start | bytes 2162696 | tf_op jit(solution)/shard_map/ppermute | solution.py:155
  54.7 3.6 %collective-permute-start.1 = (bf16[1,176,1024]{2,1,0:T(8,128)(2,1)S(1)}, bf16[1,176,1024]{2,1,0:T(8,128)(2,1)S(1)}, u32[]{:S(2)}, u32[]{:S(2)}) collective-permute-start(bf16[1,176,1024]{2,1,0:T(8,128)(2,1)S(1)} %get-tuple-element.27), channel_id=1, source_target_pairs={{0,32},{32,0},{1,33},{33,1},{2,34},{34,2},{3,35},{35,3},{4,36},{36... | collective-permute-start | bytes 1081352 | tf_op jit(solution)/shard_map/ppermute | solution.py:157
  58.3 0.9 copy-start.5
  77.3 1.1 copy-start.6
  81.9 1.0 copy-start
  82.8 1.0 copy-start.7
  83.9 19.6 %all-to-all-start.2 = ((bf16[8,64,1024]{2,1,0:T(8,128)(2,1)}), bf16[8,64,1024]{2,1,0:T(8,128)(2,1)S(1)}, u32[]{:S(2)}, u32[]{:S(2)}) async-start(bf16[8,64,1024]{2,1,0:T(8,128)(2,1)} %copy-done), calls=%async_computation.2 | async-start | bytes 2097152 | tf_op jit(solution)/shard_map/all_to_all | solution.py:202
  89.1 1.2 copy-start.8
  92.2 0.7 copy-start.1
  93.0 0.7 copy-start.3
  103.5 10.5 %copy-start.2 = (bf16[176,1024]{1,0:T(8,128)(2,1)S(1)}, bf16[176,1024]{1,0:T(8,128)(2,1)}, u32[]{:S(2)}) copy-start(bf16[176,1024]{1,0:T(8,128)(2,1)} %copy-done.1) | copy-start | bytes 1081348
  104.3 22.5 %all-to-all-start.3 = ((bf16[64,2,512]{2,1,0:T(2,128)(2,1)}), bf16[64,2,512]{2,1,0:T(2,128)(2,1)S(1)}, u32[]{:S(2)}, u32[]{:S(2)}) async-start(bf16[64,2,512]{2,1,0:T(2,128)(2,1)} %reshape.17), calls=%async_computation.3 | async-start | bytes 262144 | tf_op jit(solution)/shard_map/all_to_all | solution.py:234
  118.5 8.3 %copy-start.4 = (s32[1,64]{1,0:T(1,128)S(1)}, s32[1,64]{1,0:T(1,128)}, u32[]{:S(2)}) copy-start(s32[1,64]{1,0:T(1,128)} %picks.1) | copy-start | bytes 772

commit v3 on v2

--- a/solution.py
+++ b/solution.py
@@ -57,19 +57,21 @@
 
 def spread_kernel(rows, out, both, sems):
     count, width = both.shape[1:]
-    for i in range(2):
-        half = rows[:, 8 * i : 8 * i + 8, :].astype(F32)
-        both[i] = half.reshape(count, width).astype(BF16)
-    copies = [
-        pltpu.make_async_copy(both, out.at[i], sems.at[i]) for i in range(out.shape[0])
-    ]
-    for copy in copies:
-        copy.start()
+    values = rows[...].astype(F32)
+    copies = []
+    for kind in range(2):
+        half = values[:, 8 * kind : 8 * kind + 8, :]
+        both[kind] = half.reshape(count, width).astype(BF16)
+        for i in range(out.shape[0]):
+            copies.append(
+                pltpu.make_async_copy(both.at[kind], out.at[i, kind], sems.at[kind, i])
+            )
+            copies[-1].start()
     for copy in copies:
         copy.wait()
 
 
-def sum_kernel(parts, out):
+def sum_kernel(parts, filled, out):
     out[...] = jnp.sum(parts[...].astype(F32), 0).astype(BF16)
 
 
@@ -82,7 +84,7 @@
 
 def fill_kernel(core_ref, *refs):
     away = 1 - core_ref[0]
-    theirs, outs, sems = refs[:3], refs[6:9], refs[9]
+    theirs, (filled, *outs), sems = refs[:3], refs[6:10], refs[10]
     copies = [
         pltpu.make_async_copy(theirs[i].at[away], outs[i].at[away], sems.at[i]) for i in range(3)
     ]
@@ -90,6 +92,7 @@
         copy.start()
     for copy in copies:
         copy.wait()
+    filled[...] = jnp.ones_like(filled)
 
 
 def nt(a, b):
@@ -180,7 +183,7 @@
         out_shape=jax.ShapeDtypeStruct((batches, 2, count, width), BF16),
         scratch_shapes=[
             pltpu.VMEM((2, count, width), BF16),
-            pltpu.SemaphoreType.DMA((batches,)),
+            pltpu.SemaphoreType.DMA((2, batches)),
         ],
         compiler_params=full,
     )(rows)
@@ -215,22 +218,22 @@
         compiler_params=medium,
     )(place, acts, got)
     theirs = [lax.all_gather(send, "core", axis=0) for send in results[3:]]
-    grads = pl.pallas_call(
+    filled, *grads = pl.pallas_call(
         fill_kernel,
         in_specs=[scalar] + [near] * 3 + [far] * 3,
-        out_specs=[far] * 3,
-        out_shape=[grad] * 3,
-        input_output_aliases={4: 0, 5: 1, 6: 2},
+        out_specs=[near] + [far] * 3,
+        out_shape=[jax.ShapeDtypeStruct((8, 128), F32)] + [grad] * 3,
+        input_output_aliases={4: 1, 5: 2, 6: 3},
         scratch_shapes=[pltpu.SemaphoreType.DMA((3,))],
         compiler_params=small,
     )(place, *theirs, *results[:3])
     summed = pl.pallas_call(
         sum_kernel,
-        in_specs=[near],
+        in_specs=[near] * 2,
         out_specs=near,
         out_shape=jax.ShapeDtypeStruct((count, width), BF16),
         compiler_params=small,
-    )(parts)
+    )(parts, filled)
     returned = lax.all_to_all(
         summed.reshape(count, 2, width // 2), DEST, split_axis=0, concat_axis=0, tiled=True
     )

time: 128 us -> 128 us (level)
  blocking collectives: 46.6 us -> 69 us
  waiting for transfers between devices: 36.8 us -> 22.6 us
  starting transfers between devices: 23.8 us -> 16.8 us
  local copies, waits for them, and re-layouts: 7.62 us -> 5.48 us
    all_to_all x0 -> x1, blocking collectives: none -> 22.2 us  [shards(): lax.all_to_all(summed.reshape(count, 2, width // 2), DEST, split_axis=0,...]
    all_to_all x1 -> x0, waiting for transfers between devices: 7.27 us -> none  [shards(): lax.all_to_all(summed.reshape(count, 2, width // 2), DEST, split_axis=0,...]
    all_to_all x1 -> x0, starting transfers between devices: 7.04 us -> none  [shards(): lax.all_to_all(summed.reshape(count, 2, width // 2), DEST, split_axis=0,...]
    all_to_all x1, waiting for transfers between devices: 9.78 us -> 2.92 us  [shards(): parts = lax.all_to_all(part, BATCH, split_axis=0, concat_axis=0, tiled=True)]
    unnamed x25 -> x19, local copies, waits for them, and re-layouts: 6.69 us -> 5.2 us
  transfers between devices with their start and end apart: 5 -> 4, of which waited for: 4 -> 3; matrix products, arithmetic and copies ran while one was open for 0% -> 0% of each run, Pallas kernels for 2% -> 2%
where the time goes in v3:
time: 128 us; the launch traced here: 127 us
  blocking collectives  69 us (54%)
  waiting for transfers between devices  22.6 us (18%)
  starting transfers between devices  16.8 us (13%)
  Pallas kernels  12.1 us (9%)
  local copies, waits for them, and re-layouts  5.48 us (4%)
    all_to_all x1, blocking collectives, shards(): rows = lax.all_to_all(out, DEST, split_axis=0, concat_axis=0, tiled=True)  39.4 us
    all_to_all x1, blocking collectives, shards(): lax.all_to_all(summed.reshape(count, 2, width // 2), DEST, split_axis=0,...  22.2 us
    all_to_all x1, waiting for transfers between devices, shards(): lax.all_to_all(everyone, BATCH, split_axis=0, concat_axis=0, tiled=True)  18.1 us
    all_gather x3, blocking collectives, shards(): theirs = [lax.all_gather(send, 'core', axis=0) for send in results[3:]]  7.35 us
    all_to_all x1, starting transfers between devices, shards(): lax.all_to_all(everyone, BATCH, split_axis=0, concat_axis=0, tiled=True)  6.5 us
    all_to_all x1, starting transfers between devices, shards(): parts = lax.all_to_all(part, BATCH, split_axis=0, concat_axis=0, tiled=True)  5.22 us
    unnamed x19, local copies, waits for them, and re-layouts  5.2 us
    pallas_call x1, Pallas kernels, shards(): pl.pallas_call(products_kernel, in_specs=[near] * 4, out_specs=[near] * 2...  3.45 us
  transfers between devices with their start and end apart: 4, of which 3 were waited for; matrix products, arithmetic and copies ran while one was open for 0% of the time, Pallas kernels for 2%

profile of v3, /device:TPU:1, one launch (start us, length us, event | category | flops | bytes accessed | tf_op | source)
XLA Modules:
  0.0 127.0 jit_solution(15699044418876641173)
XLA Ops:
  0.6 2.1 %shard_map.102 = bf16[64,16,128]{2,1,0:T(8,128)(2,1)} custom-call(s32[1,64]{1,0:T(1,128)} %picks.1, f32[1,64]{1,0:T(1,128)} %gates_in.1, bf16[128,1024]{1,0:T(8,128)(2,1)} %tokens_in.1, bf16[128,1024]{1,0:T(8,128)(2,1)} %cotangent_in.1), custom_call_target="tpu_custom_call" | custom-call | tf_op jit(solution)/shard_map/pallas_call | solution.py:163
  2.7 39.4 %all_to_all.20.rows = bf16[64,16,128]{2,1,0:T(8,128)(2,1)} all-to-all(bf16[64,16,128]{2,1,0:T(8,128)(2,1)} %shard_map.102), channel_id=1, replica_groups=mesh['xh'=2,'y'=4,'core'=2,'xl'=2,'z'=16] {'core','xl','z'}, dimensions={0} | all-to-all | bytes 524288 | tf_op jit(solution)/shard_map/all_to_all | solution.py:176
  42.2 2.5 %shard_map.103 = bf16[8,2,64,1024]{3,2,1,0:T(8,128)(2,1)} custom-call(bf16[64,16,128]{2,1,0:T(8,128)(2,1)} %all_to_all.20.rows), custom_call_target="tpu_custom_call" | custom-call | tf_op jit(solution)/shard_map/pallas_call | solution.py:179
  44.7 0.0 copy-start.7
  44.7 0.0 copy-start.8
  44.8 6.5 %all-to-all-start.1 = ((bf16[8,2,64,1024]{3,2,1,0:T(8,128)(2,1)}), bf16[8,2,64,1024]{3,2,1,0:T(8,128)(2,1)S(1)}, u32[]{:S(2)}, u32[]{:S(2)}) async-start(bf16[8,2,64,1024]{3,2,1,0:T(8,128)(2,1)} %shard_map.103), calls=%async_computation.1 | async-start | bytes 4194304 | tf_op jit(solution)/shard_map/all_to_all | solution.py:190
  51.3 0.0 copy-done.7
  51.3 0.0 copy-done.8
  51.3 0.0 copy-start.6
  51.3 0.1 constant_dynamic-slice_fusion.2
  51.4 0.1 pad_maximum_fusion.1
  51.5 3.1 %collective-permute-start = (bf16[2,176,1024]{2,1,0:T(8,128)(2,1)S(1)}, bf16[2,176,1024]{2,1,0:T(8,128)(2,1)S(1)}, u32[]{:S(2)}, u32[]{:S(2)}) collective-permute-start(bf16[2,176,1024]{2,1,0:T(8,128)(2,1)S(1)} %pad_maximum_fusion.1), channel_id=1, source_target_pairs={{0,32},{32,0},{1,33},{33,1},{2,34},{34,2},{3,35},{35,3},{4,36},{36... | collective-permute-start | bytes 2162696 | tf_op jit(solution)/shard_map/ppermute | solution.py:158
  54.7 0.0 copy-done.6
  54.7 0.1 constant_dynamic-slice_fusion.1
  54.7 1.9 %collective-permute-start.1 = (bf16[1,176,1024]{2,1,0:T(8,128)(2,1)S(1)}, bf16[1,176,1024]{2,1,0:T(8,128)(2,1)S(1)}, u32[]{:S(2)}, u32[]{:S(2)}) collective-permute-start(bf16[1,176,1024]{2,1,0:T(8,128)(2,1)S(1)} %get-tuple-element.29), channel_id=1, source_target_pairs={{0,32},{32,0},{1,33},{33,1},{2,34},{34,2},{3,35},{35,3},{4,36},{36... | collective-permute-start | bytes 1081352 | tf_op jit(solution)/shard_map/ppermute | solution.py:160
  56.7 0.1 pad_maximum_fusion.own
  56.7 1.6 %collective-permute-done.1 = bf16[1,176,1024]{2,1,0:T(8,128)(2,1)S(1)} collective-permute-done((bf16[1,176,1024]{2,1,0:T(8,128)(2,1)S(1)}, bf16[1,176,1024]{2,1,0:T(8,128)(2,1)S(1)}, u32[]{:S(2)}, u32[]{:S(2)}) %collective-permute-start.1) | collective-permute-done | bytes 360480 | tf_op jit(solution)/shard_map/ppermute | solution.py:160
  58.3 0.1 pad_maximum_fusion.2.down
  58.4 0.0 collective-permute-done.other
  58.4 0.0 copy-start.2
  58.4 0.8 copy-done.2
  59.2 18.1 %all-to-all-done.1.got = bf16[8,2,64,1024]{3,2,1,0:T(8,128)(2,1)S(1)} async-done(((bf16[8,2,64,1024]{3,2,1,0:T(8,128)(2,1)}), bf16[8,2,64,1024]{3,2,1,0:T(8,128)(2,1)S(1)}, u32[]{:S(2)}, u32[]{:S(2)}) %all-to-all-start.1) | async-done | bytes 2097184 | tf_op jit(solution)/shard_map/all_to_all | solution.py:190
  77.4 0.0 copy-start.3
  77.4 1.1 copy-done.3
  78.5 3.4 %shard_map.104 = (bf16[8,64,1024]{2,1,0:T(8,128)(2,1)S(1)}, bf16[3,2,176,512]{3,2,1,0:T(8,128)(2,1)S(1)}) custom-call(bf16[8,2,64,1024]{3,2,1,0:T(8,128)(2,1)S(1)} %all-to-all-done.1.got, bf16[2,176,1024]{2,1,0:T(8,128)(2,1)S(1)} %pad_maximum_fusion.own, bf16[2,176,1024]{2,1,0:T(8,128)(2,1)S(1)} %copy-done.3, bf16[2,176,1024]{2,1,0:T(8,128)(2,1)S(1)} %pad_maximum_fusion.2.down), custom_call_target="tpu_custom_call" | custom-call | flops 1845493760 | bytes 8388608 | tf_op jit(solution)/shard_map/pallas_call | solution.py:192
  82.0 0.0 copy-start
  82.0 1.0 copy-done
  82.9 0.0 copy-start.4
  82.9 1.0 copy-done.4
  83.9 5.2 %all-to-all-start.2 = ((bf16[8,64,1024]{2,1,0:T(8,128)(2,1)}), bf16[8,64,1024]{2,1,0:T(8,128)(2,1)S(1)}, u32[]{:S(2)}, u32[]{:S(2)}) async-start(bf16[8,64,1024]{2,1,0:T(8,128)(2,1)} %copy-done), calls=%async_computation.2 | async-start | bytes 2097152 | tf_op jit(solution)/shard_map/all_to_all | solution.py:205
  89.1 0.0 copy-start.5
  89.2 1.2 copy-done.5
  90.4 1.9 %shard_map.105 = (bf16[2,176,1024]{2,1,0:T(8,128)(2,1)}, bf16[2,176,1024]{2,1,0:T(8,128)(2,1)}, bf16[2,176,1024]{2,1,0:T(8,128)(2,1)}, bf16[176,1024]{1,0:T(8,12...) custom-call(s32[1]{0:T(128)} %bitcast.core_ref, bf16[3,2,176,512]{3,2,1,0:T(8,128)(2,1)S(1)} %copy-done.5, ...), custom_call_target="tpu_custom_call" | custom-call | flops 1107296256 | bytes 6291456 | tf_op jit(solution)/shard_map/pallas_call | solution.py:209
  92.3 2.7 %all-gather = bf16[352,1024]{1,0:T(8,128)(2,1)S(1)} all-gather(bf16[176,1024]{1,0:T(8,128)(2,1)S(1)} %get-tuple-element.18), channel_id=2, replica_groups=mesh['xh'=2,'y'=4,'core'=2,'xl'=2,'z'=16] {'core'}, dimensions={0}, use_global_device_ids=true | all-gather | bytes 1081344 | tf_op jit(solution)/shard_map/all_gather | solution.py:220
  95.0 2.3 %all-gather.1 = bf16[352,1024]{1,0:T(8,128)(2,1)S(1)} all-gather(bf16[176,1024]{1,0:T(8,128)(2,1)S(1)} %get-tuple-element.19), channel_id=3, replica_groups=mesh['xh'=2,'y'=4,'core'=2,'xl'=2,'z'=16] {'core'}, dimensions={0}, use_global_device_ids=true | all-gather | bytes 1081344 | tf_op jit(solution)/shard_map/all_gather | solution.py:220
  97.3 2.3 %all-gather.2 = bf16[352,1024]{1,0:T(8,128)(2,1)S(1)} all-gather(bf16[176,1024]{1,0:T(8,128)(2,1)S(1)} %get-tuple-element.20), channel_id=4, replica_groups=mesh['xh'=2,'y'=4,'core'=2,'xl'=2,'z'=16] {'core'}, dimensions={0}, use_global_device_ids=true | all-gather | bytes 1081344 | tf_op jit(solution)/shard_map/all_gather | solution.py:220
  99.6 0.0 copy-start.1
  99.6 1.0 shard_map.106
  100.6 2.9 %all-to-all-done.2.parts = bf16[8,64,1024]{2,1,0:T(8,128)(2,1)S(1)} async-done(((bf16[8,64,1024]{2,1,0:T(8,128)(2,1)}), bf16[8,64,1024]{2,1,0:T(8,128)(2,1)S(1)}, u32[]{:S(2)}, u32[]{:S(2)}) %all-to-all-start.2) | async-done | bytes 1048608 | tf_op jit(solution)/shard_map/all_to_all | solution.py:205
  103.5 0.1 shard_map.107
  103.7 0.1 reshape.18
  103.8 22.2 %all_to_all.21 = bf16[64,2,512]{2,1,0:T(2,128)(2,1)S(1)} all-to-all(bf16[64,2,512]{2,1,0:T(2,128)(2,1)S(1)} %reshape.18), channel_id=1, replica_groups=mesh['xh'=2,'y'=4,'core'=2,'xl'=2,'z'=16] {'core','xl','z'}, dimensions={0} | all-to-all | bytes 262144 | tf_op jit(solution)/shard_map/all_to_all | solution.py:237
  126.0 0.0 copy-done.1
  126.0 1.0 shard_map.108
  (1 shorter events, 0.0 us)
Async XLA Ops:
  44.7 6.5 %copy-start.7 = (bf16[2,176,1024]{2,1,0:T(8,128)(2,1)S(1)}, bf16[2,176,1024]{2,1,0:T(8,128)(2,1)}, u32[]{:S(2)}) copy-start(bf16[2,176,1024]{2,1,0:T(8,128)(2,1)} %param.12) | copy-start | bytes 2162692
  44.7 6.5 %copy-start.8 = (bf16[2,176,1024]{2,1,0:T(8,128)(2,1)S(1)}, bf16[2,176,1024]{2,1,0:T(8,128)(2,1)}, u32[]{:S(2)}) copy-start(bf16[2,176,1024]{2,1,0:T(8,128)(2,1)} %param.11) | copy-start | bytes 2162692
  44.8 32.6 %all-to-all-start.1 = ((bf16[8,2,64,1024]{3,2,1,0:T(8,128)(2,1)}), bf16[8,2,64,1024]{3,2,1,0:T(8,128)(2,1)S(1)}, u32[]{:S(2)}, u32[]{:S(2)}) async-start(bf16[8,2,64,1024]{3,2,1,0:T(8,128)(2,1)} %shard_map.103), calls=%async_computation.1 | async-start | bytes 4194304 | tf_op jit(solution)/shard_map/all_to_all | solution.py:190
  51.3 3.4 %copy-start.6 = (bf16[2,176,1024]{2,1,0:T(8,128)(2,1)S(1)}, bf16[2,176,1024]{2,1,0:T(8,128)(2,1)}, u32[]{:S(2)}) copy-start(bf16[2,176,1024]{2,1,0:T(8,128)(2,1)} %param.13) | copy-start | bytes 2162692
  51.5 6.9 %collective-permute-start = (bf16[2,176,1024]{2,1,0:T(8,128)(2,1)S(1)}, bf16[2,176,1024]{2,1,0:T(8,128)(2,1)S(1)}, u32[]{:S(2)}, u32[]{:S(2)}) collective-permute-start(bf16[2,176,1024]{2,1,0:T(8,128)(2,1)S(1)} %pad_maximum_fusion.1), channel_id=1, source_target_pairs={{0,32},{32,0},{1,33},{33,1},{2,34},{34,2},{3,35},{35,3},{4,36},{36... | collective-permute-start | bytes 2162696 | tf_op jit(solution)/shard_map/ppermute | solution.py:158
  54.7 3.6 %collective-permute-start.1 = (bf16[1,176,1024]{2,1,0:T(8,128)(2,1)S(1)}, bf16[1,176,1024]{2,1,0:T(8,128)(2,1)S(1)}, u32[]{:S(2)}, u32[]{:S(2)}) collective-permute-start(bf16[1,176,1024]{2,1,0:T(8,128)(2,1)S(1)} %get-tuple-element.29), channel_id=1, source_target_pairs={{0,32},{32,0},{1,33},{33,1},{2,34},{34,2},{3,35},{35,3},{4,36},{36... | collective-permute-start | bytes 1081352 | tf_op jit(solution)/shard_map/ppermute | solution.py:160
  58.4 0.9 copy-start.2
  77.4 1.1 copy-start.3
  82.0 1.0 copy-start
  82.9 1.0 copy-start.4
  83.9 19.6 %all-to-all-start.2 = ((bf16[8,64,1024]{2,1,0:T(8,128)(2,1)}), bf16[8,64,1024]{2,1,0:T(8,128)(2,1)S(1)}, u32[]{:S(2)}, u32[]{:S(2)}) async-start(bf16[8,64,1024]{2,1,0:T(8,128)(2,1)} %copy-done), calls=%async_computation.2 | async-start | bytes 2097152 | tf_op jit(solution)/shard_map/all_to_all | solution.py:205
  89.1 1.2 copy-start.5
  99.6 26.4 %copy-start.1 = (s32[1,64]{1,0:T(1,128)S(1)}, s32[1,64]{1,0:T(1,128)}, u32[]{:S(2)}) copy-start(s32[1,64]{1,0:T(1,128)} %picks.1) | copy-start | bytes 772

commit v4 on v3

--- a/solution.py
+++ b/solution.py
@@ -55,20 +55,14 @@
     out[...] = scaled.reshape(out.shape).astype(BF16)
 
 
-def spread_kernel(rows, out, both, sems):
-    count, width = both.shape[1:]
+def spread_kernel(rows, weights, out):
+    batches, _, count, width = out.shape
     values = rows[...].astype(F32)
-    copies = []
     for kind in range(2):
         half = values[:, 8 * kind : 8 * kind + 8, :]
-        both[kind] = half.reshape(count, width).astype(BF16)
-        for i in range(out.shape[0]):
-            copies.append(
-                pltpu.make_async_copy(both.at[kind], out.at[i, kind], sems.at[kind, i])
-            )
-            copies[-1].start()
-    for copy in copies:
-        copy.wait()
+        half = half.reshape(count, width).astype(BF16)
+        for i in range(batches):
+            out[i, kind] = half
 
 
 def sum_kernel(parts, filled, out):
@@ -103,21 +97,21 @@
     return lax.dot_general(a, b, (((0,), (0,)), ((), ())), preferred_element_type=F32)
 
 
-def products_kernel(got, own, other, down, part, acts):
+def products_kernel(got, weights, part, acts):
     batches, _, count, width = got.shape
     x = got[:, 0].reshape(batches * count, width)
     dy = got[:, 1].reshape(batches * count, width)
-    for half, gate_up in ((0, own), (1, other)):
-        pre_gate = nt(gate_up[0], x)
-        pre_up = nt(gate_up[1], x)
-        grad_hidden = nt(down[half], dy)
+    for half in range(2):
+        pre_gate = nt(weights[half, 0], x)
+        pre_up = nt(weights[half, 1], x)
+        grad_hidden = nt(weights[half, 2], dy)
         sig = jax.nn.sigmoid(pre_gate)
         active = pre_gate * sig
         acts[0, half] = (grad_hidden * pre_up * sig * (1.0 + pre_gate * (1.0 - sig))).astype(BF16)
         acts[1, half] = (grad_hidden * active).astype(BF16)
         acts[2, half] = (active * pre_up).astype(BF16)
-    total = tn(acts[0, 0], own[0]) + tn(acts[1, 0], own[1])
-    total += tn(acts[0, 1], other[0]) + tn(acts[1, 1], other[1])
+    total = tn(acts[0, 0], weights[0, 0]) + tn(acts[1, 0], weights[0, 1])
+    total += tn(acts[0, 1], weights[1, 0]) + tn(acts[1, 1], weights[1, 1])
     part[...] = total.astype(BF16).reshape(part.shape)
 
 
@@ -154,10 +148,17 @@
             [lax.dynamic_index_in_dim(w, expert, 0, keepdims=False) for w in arrays]
         )
 
-    own = of(core, w_gate, w_up)
-    other = lax.ppermute(of(1 - core, w_gate, w_up), "core", SWAP)
-    down = jnp.concatenate(
-        [of(core, w_down), lax.ppermute(of(1 - core, w_down), "core", SWAP)], 0
+    halves = jnp.stack(
+        [
+            of(core, w_gate, w_up, w_down),
+            jnp.concatenate(
+                [
+                    lax.ppermute(of(1 - core, *arrays), "core", SWAP)
+                    for arrays in ((w_gate, w_up), (w_down,))
+                ],
+                0,
+            ),
+        ]
     )
 
     out = pl.pallas_call(
@@ -178,20 +179,16 @@
     sources = batches * count
     everyone = pl.pallas_call(
         spread_kernel,
-        in_specs=[near],
-        out_specs=far,
+        in_specs=[near, far],
+        out_specs=near,
         out_shape=jax.ShapeDtypeStruct((batches, 2, count, width), BF16),
-        scratch_shapes=[
-            pltpu.VMEM((2, count, width), BF16),
-            pltpu.SemaphoreType.DMA((2, batches)),
-        ],
-        compiler_params=full,
-    )(rows)
+        compiler_params=small,
+    )(rows, halves)
     got = lax.all_to_all(everyone, BATCH, split_axis=0, concat_axis=0, tiled=True)
 
     part, acts = pl.pallas_call(
         products_kernel,
-        in_specs=[near] * 4,
+        in_specs=[near] * 2,
         out_specs=[near] * 2,
         out_shape=[
             jax.ShapeDtypeStruct((batches, count, width), BF16),
@@ -201,7 +198,7 @@
             flops=20 * sources * units * width, bytes_accessed=8 * 2**20, transcendentals=0
         ),
         compiler_params=medium,
-    )(got, own, other, down)
+    )(got, halves)
     parts = lax.all_to_all(part, BATCH, split_axis=0, concat_axis=0, tiled=True)
 
     side = jax.ShapeDtypeStruct((units, width), BF16)

time: 128 us -> 124 us (0.969)
  starting transfers between devices: 16.8 us -> 26.3 us
  waiting for transfers between devices: 22.6 us -> 14.9 us
  blocking collectives: 69 us -> 66.1 us
  Pallas kernels: 12.1 us -> 9.8 us
    all_to_all x1, starting transfers between devices: 6.5 us -> 18.2 us  [shards(): rows = lax.all_to_all(out, DEST, split_axis=0, concat_axis=0, tiled=True)]
    all_to_all x1, blocking collectives: 39.4 us -> 32.7 us  [shards(): lax.all_to_all(everyone, BATCH, split_axis=0, concat_axis=0, tiled=True)]
    all_to_all x1, waiting for transfers between devices: 18.1 us -> 13.5 us  [shards(): rows = lax.all_to_all(out, DEST, split_axis=0, concat_axis=0, tiled=True)]
    all_to_all x1, waiting for transfers between devices: 2.92 us -> 0.01 us  [shards(): parts = lax.all_to_all(part, BATCH, split_axis=0, concat_axis=0, tiled=True)]
    pallas_call x2, Pallas kernels: 5.99 us -> 3.59 us  [the longest x1 3.44 us: shards(): pl.pallas_call(products_kernel, in_specs=[near] * 2, out_specs=[near] * 2...]
    all_gather x3, blocking collectives: 7.35 us -> 9.36 us  [shards(): theirs = [lax.all_gather(send, 'core', axis=0) for send in results[3:]]]
    unnamed x19 -> x17, local copies, waits for them, and re-layouts: 5.2 us -> 3.24 us
    all_to_all x1, blocking collectives: 22.2 us -> 24.1 us  [shards(): lax.all_to_all(summed.reshape(count, 2, width // 2), DEST, split_axis=0,...]
  transfers between devices with their start and end apart: 4 -> 4, of which waited for: 3 -> 2; matrix products, arithmetic and copies ran while one was open for 0% -> 1% of each run, Pallas kernels for 2% -> 2%
where the time goes in v4:
time: 124 us; the launch traced here: 123 us
  blocking collectives  66.1 us (53%)
  starting transfers between devices  26.3 us (21%)
  waiting for transfers between devices  14.9 us (12%)
  Pallas kernels  9.8 us (8%)
  local copies, waits for them, and re-layouts  4.58 us (4%)
    all_to_all x1, blocking collectives, shards(): lax.all_to_all(everyone, BATCH, split_axis=0, concat_axis=0, tiled=True)  32.7 us
    all_to_all x1, blocking collectives, shards(): lax.all_to_all(summed.reshape(count, 2, width // 2), DEST, split_axis=0,...  24.1 us
    all_to_all x1, starting transfers between devices, shards(): rows = lax.all_to_all(out, DEST, split_axis=0, concat_axis=0, tiled=True)  18.2 us
    all_to_all x1, waiting for transfers between devices, shards(): rows = lax.all_to_all(out, DEST, split_axis=0, concat_axis=0, tiled=True)  13.5 us
    all_gather x3, blocking collectives, shards(): theirs = [lax.all_gather(send, 'core', axis=0) for send in results[3:]]  9.36 us
    ppermute x2, starting transfers between devices, shards(): lax.ppermute(of(1 - core, *arrays), 'core', SWAP)  4.46 us
    all_to_all x1, starting transfers between devices, shards(): parts = lax.all_to_all(part, BATCH, split_axis=0, concat_axis=0, tiled=True)  3.69 us
    pallas_call x1, Pallas kernels, shards(): pl.pallas_call(products_kernel, in_specs=[near] * 2, out_specs=[near] * 2...  3.44 us
  transfers between devices with their start and end apart: 4, of which 2 were waited for; matrix products, arithmetic and copies ran while one was open for 1% of the time, Pallas kernels for 2%

profile of v4, /device:TPU:1, one launch (start us, length us, event | category | flops | bytes accessed | tf_op | source)
XLA Modules:
  0.0 123.0 jit_solution(14496427223463277085)
XLA Ops:
  0.6 0.0 copy-start.7
  0.6 2.2 %shard_map.102 = bf16[64,16,128]{2,1,0:T(8,128)(2,1)} custom-call(s32[1,64]{1,0:T(1,128)} %picks.1, f32[1,64]{1,0:T(1,128)} %gates_in.1, bf16[128,1024]{1,0:T(8,128)(2,1)} %tokens_in.1, bf16[128,1024]{1,0:T(8,128)(2,1)} %cotangent_in.1), custom_call_target="tpu_custom_call" | custom-call | tf_op jit(solution)/shard_map/pallas_call | solution.py:164
  2.8 18.2 %all-to-all-start = ((bf16[64,16,128]{2,1,0:T(8,128)(2,1)}), bf16[64,16,128]{2,1,0:T(8,128)(2,1)S(1)}, u32[]{:S(2)}, u32[]{:S(2)}) async-start(bf16[64,16,128]{2,1,0:T(8,128)(2,1)} %shard_map.102), calls=%async_computation | async-start | bytes 524288 | tf_op jit(solution)/shard_map/all_to_all | solution.py:177
  21.0 0.0 copy-done.7
  21.0 1.2 constant_dynamic-slice_fusion.4
  22.2 0.0 copy-start.6
  22.2 0.1 pad_maximum_fusion.1
  22.3 2.4 %collective-permute-start = (bf16[2,176,1024]{2,1,0:T(8,128)(2,1)S(1)}, bf16[2,176,1024]{2,1,0:T(8,128)(2,1)S(1)}, u32[]{:S(2)}, u32[]{:S(2)}) collective-permute-start(bf16[2,176,1024]{2,1,0:T(8,128)(2,1)S(1)} %pad_maximum_fusion.1), channel_id=1, source_target_pairs={{0,32},{32,0},{1,33},{33,1},{2,34},{34,2},{3,35},{35,3},{4,36},{36... | collective-permute-start | bytes 2162696 | tf_op jit(solution)/shard_map/ppermute | solution.py:156
  24.7 0.0 copy-done.6
  24.7 0.1 constant_dynamic-slice_fusion.3
  24.8 2.1 %collective-permute-start.1 = (bf16[1,176,1024]{2,1,0:T(8,128)(2,1)S(1)}, bf16[1,176,1024]{2,1,0:T(8,128)(2,1)S(1)}, u32[]{:S(2)}, u32[]{:S(2)}) collective-permute-start(bf16[1,176,1024]{2,1,0:T(8,128)(2,1)S(1)} %get-tuple-element.33), channel_id=1, source_target_pairs={{0,32},{32,0},{1,33},{33,1},{2,34},{34,2},{3,35},{35,3},{4,36},{36... | collective-permute-start | bytes 1081352 | tf_op jit(solution)/shard_map/ppermute | solution.py:156
  26.9 0.1 maximum_bitcast_fusion
  27.0 1.4 %collective-permute-done.1 = bf16[1,176,1024]{2,1,0:T(8,128)(2,1)S(1)} collective-permute-done((bf16[1,176,1024]{2,1,0:T(8,128)(2,1)S(1)}, bf16[1,176,1024]{2,1,0:T(8,128)(2,1)S(1)}, u32[]{:S(2)}, u32[]{:S(2)}) %collective-permute-start.1) | collective-permute-done | bytes 360480 | tf_op jit(solution)/shard_map/ppermute | solution.py:156
  28.4 0.0 collective-permute-done
  28.4 0.1 maximum_bitcast_fusion.1
  28.5 0.2 pad_maximum_fusion.weights
  28.7 13.5 %all-to-all-done.rows = bf16[64,16,128]{2,1,0:T(8,128)(2,1)S(1)} async-done(((bf16[64,16,128]{2,1,0:T(8,128)(2,1)}), bf16[64,16,128]{2,1,0:T(8,128)(2,1)S(1)}, u32[]{:S(2)}, u32[]{:S(2)}) %all-to-all-start) | async-done | bytes 262176 | tf_op jit(solution)/shard_map/all_to_all | solution.py:177
  42.2 0.1 shard_map.103
  42.3 32.7 %all_to_all.20.got = bf16[8,2,64,1024]{3,2,1,0:T(8,128)(2,1)S(1)} all-to-all(bf16[8,2,64,1024]{3,2,1,0:T(8,128)(2,1)S(1)} %shard_map.103), channel_id=1, replica_groups=mesh['xh'=2,'y'=4,'core'=2,'xl'=2,'z'=16] {'xh','y'}, dimensions={0} | all-to-all | bytes 4194304 | tf_op jit(solution)/shard_map/all_to_all | solution.py:187
  75.0 0.0 copy-start
  75.0 3.4 %shard_map.104 = (bf16[8,64,1024]{2,1,0:T(8,128)(2,1)S(1)}, bf16[3,2,176,512]{3,2,1,0:T(8,128)(2,1)S(1)}) custom-call(bf16[8,2,64,1024]{3,2,1,0:T(8,128)(2,1)S(1)} %all_to_all.20.got, bf16[2,3,176,1024]{3,2,1,0:T(8,128)(2,1)S(1)} %pad_maximum_fusion.weights), custom_call_target="tpu_custom_call" | custom-call | flops 1845493760 | bytes 8388608 | tf_op jit(solution)/shard_map/pallas_call | solution.py:189
  78.5 0.0 copy-done
  78.5 0.0 copy-start.2
  78.5 1.0 copy-done.2
  79.5 0.0 copy-start.4
  79.5 1.0 copy-done.4
  80.4 0.0 copy-start.1
  80.4 3.7 %all-to-all-start.2 = ((bf16[8,64,1024]{2,1,0:T(8,128)(2,1)}), bf16[8,64,1024]{2,1,0:T(8,128)(2,1)S(1)}, u32[]{:S(2)}, u32[]{:S(2)}) async-start(bf16[8,64,1024]{2,1,0:T(8,128)(2,1)} %copy-done.2), calls=%async_computation.2 | async-start | bytes 2097152 | tf_op jit(solution)/shard_map/all_to_all | solution.py:202
  84.1 0.0 copy-done.1
  84.2 0.0 copy-start.5
  84.2 1.2 copy-done.5
  85.4 1.9 %shard_map.105 = (bf16[2,176,1024]{2,1,0:T(8,128)(2,1)}, bf16[2,176,1024]{2,1,0:T(8,128)(2,1)}, bf16[2,176,1024]{2,1,0:T(8,128)(2,1)}, bf16[176,1024]{1,0:T(8,12...) custom-call(s32[1]{0:T(128)} %bitcast.2.core_ref, bf16[3,2,176,512]{3,2,1,0:T(8,128)(2,1)S(1)} %copy-done.5, ...), custom_call_target="tpu_custom_call" | custom-call | flops 1107296256 | bytes 6291456 | tf_op jit(solution)/shard_map/pallas_call | solution.py:206
  87.3 4.7 %all-gather = bf16[352,1024]{1,0:T(8,128)(2,1)S(1)} all-gather(bf16[176,1024]{1,0:T(8,128)(2,1)S(1)} %get-tuple-element.18), channel_id=2, replica_groups=mesh['xh'=2,'y'=4,'core'=2,'xl'=2,'z'=16] {'core'}, dimensions={0}, use_global_device_ids=true | all-gather | bytes 1081344 | tf_op jit(solution)/shard_map/all_gather | solution.py:217
  92.0 2.3 %all-gather.1 = bf16[352,1024]{1,0:T(8,128)(2,1)S(1)} all-gather(bf16[176,1024]{1,0:T(8,128)(2,1)S(1)} %get-tuple-element.19), channel_id=3, replica_groups=mesh['xh'=2,'y'=4,'core'=2,'xl'=2,'z'=16] {'core'}, dimensions={0}, use_global_device_ids=true | all-gather | bytes 1081344 | tf_op jit(solution)/shard_map/all_gather | solution.py:217
  94.3 2.3 %all-gather.2 = bf16[352,1024]{1,0:T(8,128)(2,1)S(1)} all-gather(bf16[176,1024]{1,0:T(8,128)(2,1)S(1)} %get-tuple-element.20), channel_id=4, replica_groups=mesh['xh'=2,'y'=4,'core'=2,'xl'=2,'z'=16] {'core'}, dimensions={0}, use_global_device_ids=true | all-gather | bytes 1081344 | tf_op jit(solution)/shard_map/all_gather | solution.py:217
  96.6 1.0 shard_map.106
  97.6 0.0 copy-start.3
  97.7 0.0 all-to-all-done.2.parts
  97.7 0.1 shard_map.107
  97.8 0.1 reshape.18
  97.9 24.1 %all_to_all.21 = bf16[64,2,512]{2,1,0:T(2,128)(2,1)S(1)} all-to-all(bf16[64,2,512]{2,1,0:T(2,128)(2,1)S(1)} %reshape.18), channel_id=1, replica_groups=mesh['xh'=2,'y'=4,'core'=2,'xl'=2,'z'=16] {'core','xl','z'}, dimensions={0} | all-to-all | bytes 262144 | tf_op jit(solution)/shard_map/all_to_all | solution.py:234
  122.0 0.0 copy-done.3
  122.0 1.0 shard_map.108
  (1 shorter events, 0.0 us)
Async XLA Ops:
  0.6 20.4 %copy-start.7 = (bf16[2,176,1024]{2,1,0:T(8,128)(2,1)S(1)}, bf16[2,176,1024]{2,1,0:T(8,128)(2,1)}, u32[]{:S(2)}) copy-start(bf16[2,176,1024]{2,1,0:T(8,128)(2,1)} %param.12) | copy-start | bytes 2162692
  2.8 39.4 %all-to-all-start = ((bf16[64,16,128]{2,1,0:T(8,128)(2,1)}), bf16[64,16,128]{2,1,0:T(8,128)(2,1)S(1)}, u32[]{:S(2)}, u32[]{:S(2)}) async-start(bf16[64,16,128]{2,1,0:T(8,128)(2,1)} %shard_map.102), calls=%async_computation | async-start | bytes 524288 | tf_op jit(solution)/shard_map/all_to_all | solution.py:177
  22.2 2.5 %copy-start.6 = (bf16[2,176,1024]{2,1,0:T(8,128)(2,1)S(1)}, bf16[2,176,1024]{2,1,0:T(8,128)(2,1)}, u32[]{:S(2)}) copy-start(bf16[2,176,1024]{2,1,0:T(8,128)(2,1)} %param.13) | copy-start | bytes 2162692
  22.3 6.1 %collective-permute-start = (bf16[2,176,1024]{2,1,0:T(8,128)(2,1)S(1)}, bf16[2,176,1024]{2,1,0:T(8,128)(2,1)S(1)}, u32[]{:S(2)}, u32[]{:S(2)}) collective-permute-start(bf16[2,176,1024]{2,1,0:T(8,128)(2,1)S(1)} %pad_maximum_fusion.1), channel_id=1, source_target_pairs={{0,32},{32,0},{1,33},{33,1},{2,34},{34,2},{3,35},{35,3},{4,36},{36... | collective-permute-start | bytes 2162696 | tf_op jit(solution)/shard_map/ppermute | solution.py:156
  24.8 3.6 %collective-permute-start.1 = (bf16[1,176,1024]{2,1,0:T(8,128)(2,1)S(1)}, bf16[1,176,1024]{2,1,0:T(8,128)(2,1)S(1)}, u32[]{:S(2)}, u32[]{:S(2)}) collective-permute-start(bf16[1,176,1024]{2,1,0:T(8,128)(2,1)S(1)} %get-tuple-element.33), channel_id=1, source_target_pairs={{0,32},{32,0},{1,33},{33,1},{2,34},{34,2},{3,35},{35,3},{4,36},{36... | collective-permute-start | bytes 1081352 | tf_op jit(solution)/shard_map/ppermute | solution.py:156
  75.0 3.5 %copy-start = (bf16[8,2,64,1024]{3,2,1,0:T(8,128)(2,1)}, bf16[8,2,64,1024]{3,2,1,0:T(8,128)(2,1)S(1)}, u32[]{:S(2)}) copy-start(bf16[8,2,64,1024]{3,2,1,0:T(8,128)(2,1)S(1)} %all_to_all.20.got) | copy-start | bytes 6291460
  78.5 1.0 copy-start.2
  79.5 1.0 copy-start.4
  80.4 3.7 %copy-start.1 = (bf16[8,2,64,1024]{3,2,1,0:T(8,128)(2,1)S(1)}, bf16[8,2,64,1024]{3,2,1,0:T(8,128)(2,1)}, u32[]{:S(2)}) copy-start(bf16[8,2,64,1024]{3,2,1,0:T(8,128)(2,1)} %copy-done) | copy-start | bytes 6291460
  80.4 17.2 %all-to-all-start.2 = ((bf16[8,64,1024]{2,1,0:T(8,128)(2,1)}), bf16[8,64,1024]{2,1,0:T(8,128)(2,1)S(1)}, u32[]{:S(2)}, u32[]{:S(2)}) async-start(bf16[8,64,1024]{2,1,0:T(8,128)(2,1)} %copy-done.2), calls=%async_computation.2 | async-start | bytes 2097152 | tf_op jit(solution)/shard_map/all_to_all | solution.py:202
  84.2 1.2 %copy-start.5 = (bf16[3,2,176,512]{3,2,1,0:T(8,128)(2,1)S(1)}, bf16[3,2,176,512]{3,2,1,0:T(8,128)(2,1)}, u32[]{:S(2)}) copy-start(bf16[3,2,176,512]{3,2,1,0:T(8,128)(2,1)} %copy-done.4) | copy-start | bytes 3244036
  97.6 24.3 %copy-start.3 = (s32[1,64]{1,0:T(1,128)S(1)}, s32[1,64]{1,0:T(1,128)}, u32[]{:S(2)}) copy-start(s32[1,64]{1,0:T(1,128)} %picks.1) | copy-start | bytes 772

commit v5 on v4

--- a/solution.py
+++ b/solution.py
@@ -7,7 +7,7 @@
 
 AXES = ("xh", "y", "core", "xl", "z")
 DEST = ("core", "xl", "z")
-BATCH = ("xh", "y")
+BATCH = ("y", "xh")
 SWAP = ((0, 1), (1, 0))
 F32, BF16 = jnp.float32, jnp.bfloat16
 

time: 124 us -> 125 us (level)
  waiting for transfers between devices: 14.9 us -> 16.4 us
    all_to_all x1, waiting for transfers between devices: 0.01 us -> 1.55 us  [shards(): parts = lax.all_to_all(part, BATCH, split_axis=0, concat_axis=0, tiled=True)]
  transfers between devices with their start and end apart: 4 -> 4, of which waited for: 2 -> 3; matrix products, arithmetic and copies ran while one was open for 1% -> 1% of each run, Pallas kernels for 2% -> 2%
where the time goes in v5:
time: 125 us
  blocking collectives  66.3 us (53%)
  starting transfers between devices  26.3 us (21%)
  waiting for transfers between devices  16.4 us (13%)
  Pallas kernels  9.79 us (8%)
  local copies, waits for them, and re-layouts  4.59 us (4%)
    all_to_all x1, blocking collectives, shards(): lax.all_to_all(everyone, BATCH, split_axis=0, concat_axis=0, tiled=True)  33.1 us
    all_to_all x1, blocking collectives, shards(): lax.all_to_all(summed.reshape(count, 2, width // 2), DEST, split_axis=0,...  24.2 us
    all_to_all x1, starting transfers between devices, shards(): rows = lax.all_to_all(out, DEST, split_axis=0, concat_axis=0, tiled=True)  18.2 us
    all_to_all x1, waiting for transfers between devices, shards(): rows = lax.all_to_all(out, DEST, split_axis=0, concat_axis=0, tiled=True)  13.5 us
    all_gather x3, blocking collectives, shards(): theirs = [lax.all_gather(send, 'core', axis=0) for send in results[3:]]  9.02 us
    ppermute x2, starting transfers between devices, shards(): lax.ppermute(of(1 - core, *arrays), 'core', SWAP)  4.46 us
    all_to_all x1, starting transfers between devices, shards(): parts = lax.all_to_all(part, BATCH, split_axis=0, concat_axis=0, tiled=True)  3.69 us
    pallas_call x1, Pallas kernels, shards(): pl.pallas_call(products_kernel, in_specs=[near] * 2, out_specs=[near] * 2...  3.44 us
  transfers between devices with their start and end apart: 4, of which 3 were waited for; matrix products, arithmetic and copies ran while one was open for 1% of the time, Pallas kernels for 2%

profile of v5, /device:TPU:1, one launch (start us, length us, event | category | flops | bytes accessed | tf_op | source)
XLA Modules:
  0.0 124.8 jit_solution(17998820165045452922)
XLA Ops:
  0.6 0.0 copy-start.7
  0.6 2.2 %shard_map.102 = bf16[64,16,128]{2,1,0:T(8,128)(2,1)} custom-call(s32[1,64]{1,0:T(1,128)} %picks.1, f32[1,64]{1,0:T(1,128)} %gates_in.1, bf16[128,1024]{1,0:T(8,128)(2,1)} %tokens_in.1, bf16[128,1024]{1,0:T(8,128)(2,1)} %cotangent_in.1), custom_call_target="tpu_custom_call" | custom-call | tf_op jit(solution)/shard_map/pallas_call | solution.py:164
  2.8 18.2 %all-to-all-start = ((bf16[64,16,128]{2,1,0:T(8,128)(2,1)}), bf16[64,16,128]{2,1,0:T(8,128)(2,1)S(1)}, u32[]{:S(2)}, u32[]{:S(2)}) async-start(bf16[64,16,128]{2,1,0:T(8,128)(2,1)} %shard_map.102), calls=%async_computation | async-start | bytes 524288 | tf_op jit(solution)/shard_map/all_to_all | solution.py:177
  21.0 0.0 copy-done.7
  21.0 1.2 constant_dynamic-slice_fusion.4
  22.2 0.0 copy-start.6
  22.2 0.1 pad_maximum_fusion.1
  22.3 2.4 %collective-permute-start = (bf16[2,176,1024]{2,1,0:T(8,128)(2,1)S(1)}, bf16[2,176,1024]{2,1,0:T(8,128)(2,1)S(1)}, u32[]{:S(2)}, u32[]{:S(2)}) collective-permute-start(bf16[2,176,1024]{2,1,0:T(8,128)(2,1)S(1)} %pad_maximum_fusion.1), channel_id=1, source_target_pairs={{0,32},{32,0},{1,33},{33,1},{2,34},{34,2},{3,35},{35,3},{4,36},{36... | collective-permute-start | bytes 2162696 | tf_op jit(solution)/shard_map/ppermute | solution.py:156
  24.7 0.0 copy-done.6
  24.7 0.1 constant_dynamic-slice_fusion.3
  24.8 2.1 %collective-permute-start.1 = (bf16[1,176,1024]{2,1,0:T(8,128)(2,1)S(1)}, bf16[1,176,1024]{2,1,0:T(8,128)(2,1)S(1)}, u32[]{:S(2)}, u32[]{:S(2)}) collective-permute-start(bf16[1,176,1024]{2,1,0:T(8,128)(2,1)S(1)} %get-tuple-element.33), channel_id=1, source_target_pairs={{0,32},{32,0},{1,33},{33,1},{2,34},{34,2},{3,35},{35,3},{4,36},{36... | collective-permute-start | bytes 1081352 | tf_op jit(solution)/shard_map/ppermute | solution.py:156
  26.9 0.1 maximum_bitcast_fusion
  27.0 1.4 %collective-permute-done.1 = bf16[1,176,1024]{2,1,0:T(8,128)(2,1)S(1)} collective-permute-done((bf16[1,176,1024]{2,1,0:T(8,128)(2,1)S(1)}, bf16[1,176,1024]{2,1,0:T(8,128)(2,1)S(1)}, u32[]{:S(2)}, u32[]{:S(2)}) %collective-permute-start.1) | collective-permute-done | bytes 360480 | tf_op jit(solution)/shard_map/ppermute | solution.py:156
  28.4 0.0 collective-permute-done
  28.4 0.1 maximum_bitcast_fusion.1
  28.5 0.2 pad_maximum_fusion.weights
  28.7 13.5 %all-to-all-done.rows = bf16[64,16,128]{2,1,0:T(8,128)(2,1)S(1)} async-done(((bf16[64,16,128]{2,1,0:T(8,128)(2,1)}), bf16[64,16,128]{2,1,0:T(8,128)(2,1)S(1)}, u32[]{:S(2)}, u32[]{:S(2)}) %all-to-all-start) | async-done | bytes 262176 | tf_op jit(solution)/shard_map/all_to_all | solution.py:177
  42.2 0.1 shard_map.103
  42.3 33.1 %all_to_all.20.got = bf16[8,2,64,1024]{3,2,1,0:T(8,128)(2,1)S(1)} all-to-all(bf16[8,2,64,1024]{3,2,1,0:T(8,128)(2,1)S(1)} %shard_map.103), channel_id=1, replica_groups=mesh['xh'=2,'y'=4,'core'=2,'xl'=2,'z'=16] {'y','xh'}, dimensions={0} | all-to-all | bytes 4194304 | tf_op jit(solution)/shard_map/all_to_all | solution.py:187
  75.4 0.0 copy-start
  75.4 3.4 %shard_map.104 = (bf16[8,64,1024]{2,1,0:T(8,128)(2,1)S(1)}, bf16[3,2,176,512]{3,2,1,0:T(8,128)(2,1)S(1)}) custom-call(bf16[8,2,64,1024]{3,2,1,0:T(8,128)(2,1)S(1)} %all_to_all.20.got, bf16[2,3,176,1024]{3,2,1,0:T(8,128)(2,1)S(1)} %pad_maximum_fusion.weights), custom_call_target="tpu_custom_call" | custom-call | flops 1845493760 | bytes 8388608 | tf_op jit(solution)/shard_map/pallas_call | solution.py:189
  78.9 0.0 copy-done
  78.9 0.0 copy-start.2
  78.9 1.0 copy-done.2
  79.9 0.0 copy-start.4
  79.9 1.0 copy-done.4
  80.8 0.0 copy-start.1
  80.9 3.7 %all-to-all-start.2 = ((bf16[8,64,1024]{2,1,0:T(8,128)(2,1)}), bf16[8,64,1024]{2,1,0:T(8,128)(2,1)S(1)}, u32[]{:S(2)}, u32[]{:S(2)}) async-start(bf16[8,64,1024]{2,1,0:T(8,128)(2,1)} %copy-done.2), calls=%async_computation.2 | async-start | bytes 2097152 | tf_op jit(solution)/shard_map/all_to_all | solution.py:202
  84.5 0.0 copy-done.1
  84.6 0.0 copy-start.5
  84.6 1.2 copy-done.5
  85.8 1.9 %shard_map.105 = (bf16[2,176,1024]{2,1,0:T(8,128)(2,1)}, bf16[2,176,1024]{2,1,0:T(8,128)(2,1)}, bf16[2,176,1024]{2,1,0:T(8,128)(2,1)}, bf16[176,1024]{1,0:T(8,12...) custom-call(s32[1]{0:T(128)} %bitcast.2.core_ref, bf16[3,2,176,512]{3,2,1,0:T(8,128)(2,1)S(1)} %copy-done.5, ...), custom_call_target="tpu_custom_call" | custom-call | flops 1107296256 | bytes 6291456 | tf_op jit(solution)/shard_map/pallas_call | solution.py:206
  87.7 4.4 %all-gather = bf16[352,1024]{1,0:T(8,128)(2,1)S(1)} all-gather(bf16[176,1024]{1,0:T(8,128)(2,1)S(1)} %get-tuple-element.18), channel_id=2, replica_groups=mesh['xh'=2,'y'=4,'core'=2,'xl'=2,'z'=16] {'core'}, dimensions={0}, use_global_device_ids=true | all-gather | bytes 1081344 | tf_op jit(solution)/shard_map/all_gather | solution.py:217
  92.1 2.3 %all-gather.1 = bf16[352,1024]{1,0:T(8,128)(2,1)S(1)} all-gather(bf16[176,1024]{1,0:T(8,128)(2,1)S(1)} %get-tuple-element.19), channel_id=3, replica_groups=mesh['xh'=2,'y'=4,'core'=2,'xl'=2,'z'=16] {'core'}, dimensions={0}, use_global_device_ids=true | all-gather | bytes 1081344 | tf_op jit(solution)/shard_map/all_gather | solution.py:217
  94.4 2.3 %all-gather.2 = bf16[352,1024]{1,0:T(8,128)(2,1)S(1)} all-gather(bf16[176,1024]{1,0:T(8,128)(2,1)S(1)} %get-tuple-element.20), channel_id=4, replica_groups=mesh['xh'=2,'y'=4,'core'=2,'xl'=2,'z'=16] {'core'}, dimensions={0}, use_global_device_ids=true | all-gather | bytes 1081344 | tf_op jit(solution)/shard_map/all_gather | solution.py:217
  96.7 1.0 shard_map.106
  97.7 0.0 copy-start.3
  97.7 1.6 %all-to-all-done.2.parts = bf16[8,64,1024]{2,1,0:T(8,128)(2,1)S(1)} async-done(((bf16[8,64,1024]{2,1,0:T(8,128)(2,1)}), bf16[8,64,1024]{2,1,0:T(8,128)(2,1)S(1)}, u32[]{:S(2)}, u32[]{:S(2)}) %all-to-all-start.2) | async-done | bytes 1048608 | tf_op jit(solution)/shard_map/all_to_all | solution.py:202
  99.3 0.1 shard_map.107
  99.4 0.1 reshape.18
  99.5 24.2 %all_to_all.21 = bf16[64,2,512]{2,1,0:T(2,128)(2,1)S(1)} all-to-all(bf16[64,2,512]{2,1,0:T(2,128)(2,1)S(1)} %reshape.18), channel_id=1, replica_groups=mesh['xh'=2,'y'=4,'core'=2,'xl'=2,'z'=16] {'core','xl','z'}, dimensions={0} | all-to-all | bytes 262144 | tf_op jit(solution)/shard_map/all_to_all | solution.py:234
  123.7 0.0 copy-done.3
  123.7 1.0 shard_map.108
  (1 shorter events, 0.0 us)
Async XLA Ops:
  0.6 20.4 %copy-start.7 = (bf16[2,176,1024]{2,1,0:T(8,128)(2,1)S(1)}, bf16[2,176,1024]{2,1,0:T(8,128)(2,1)}, u32[]{:S(2)}) copy-start(bf16[2,176,1024]{2,1,0:T(8,128)(2,1)} %param.12) | copy-start | bytes 2162692
  2.8 39.4 %all-to-all-start = ((bf16[64,16,128]{2,1,0:T(8,128)(2,1)}), bf16[64,16,128]{2,1,0:T(8,128)(2,1)S(1)}, u32[]{:S(2)}, u32[]{:S(2)}) async-start(bf16[64,16,128]{2,1,0:T(8,128)(2,1)} %shard_map.102), calls=%async_computation | async-start | bytes 524288 | tf_op jit(solution)/shard_map/all_to_all | solution.py:177
  22.2 2.5 %copy-start.6 = (bf16[2,176,1024]{2,1,0:T(8,128)(2,1)S(1)}, bf16[2,176,1024]{2,1,0:T(8,128)(2,1)}, u32[]{:S(2)}) copy-start(bf16[2,176,1024]{2,1,0:T(8,128)(2,1)} %param.13) | copy-start | bytes 2162692
  22.3 6.1 %collective-permute-start = (bf16[2,176,1024]{2,1,0:T(8,128)(2,1)S(1)}, bf16[2,176,1024]{2,1,0:T(8,128)(2,1)S(1)}, u32[]{:S(2)}, u32[]{:S(2)}) collective-permute-start(bf16[2,176,1024]{2,1,0:T(8,128)(2,1)S(1)} %pad_maximum_fusion.1), channel_id=1, source_target_pairs={{0,32},{32,0},{1,33},{33,1},{2,34},{34,2},{3,35},{35,3},{4,36},{36... | collective-permute-start | bytes 2162696 | tf_op jit(solution)/shard_map/ppermute | solution.py:156
  24.8 3.6 %collective-permute-start.1 = (bf16[1,176,1024]{2,1,0:T(8,128)(2,1)S(1)}, bf16[1,176,1024]{2,1,0:T(8,128)(2,1)S(1)}, u32[]{:S(2)}, u32[]{:S(2)}) collective-permute-start(bf16[1,176,1024]{2,1,0:T(8,128)(2,1)S(1)} %get-tuple-element.33), channel_id=1, source_target_pairs={{0,32},{32,0},{1,33},{33,1},{2,34},{34,2},{3,35},{35,3},{4,36},{36... | collective-permute-start | bytes 1081352 | tf_op jit(solution)/shard_map/ppermute | solution.py:156
  75.4 3.5 %copy-start = (bf16[8,2,64,1024]{3,2,1,0:T(8,128)(2,1)}, bf16[8,2,64,1024]{3,2,1,0:T(8,128)(2,1)S(1)}, u32[]{:S(2)}) copy-start(bf16[8,2,64,1024]{3,2,1,0:T(8,128)(2,1)S(1)} %all_to_all.20.got) | copy-start | bytes 6291460
  78.9 1.0 copy-start.2
  79.9 1.0 copy-start.4
  80.8 3.7 %copy-start.1 = (bf16[8,2,64,1024]{3,2,1,0:T(8,128)(2,1)S(1)}, bf16[8,2,64,1024]{3,2,1,0:T(8,128)(2,1)}, u32[]{:S(2)}) copy-start(bf16[8,2,64,1024]{3,2,1,0:T(8,128)(2,1)} %copy-done) | copy-start | bytes 6291460
  80.9 18.4 %all-to-all-start.2 = ((bf16[8,64,1024]{2,1,0:T(8,128)(2,1)}), bf16[8,64,1024]{2,1,0:T(8,128)(2,1)S(1)}, u32[]{:S(2)}, u32[]{:S(2)}) async-start(bf16[8,64,1024]{2,1,0:T(8,128)(2,1)} %copy-done.2), calls=%async_computation.2 | async-start | bytes 2097152 | tf_op jit(solution)/shard_map/all_to_all | solution.py:202
  84.6 1.2 copy-start.5
  97.7 26.0 %copy-start.3 = (s32[1,64]{1,0:T(1,128)S(1)}, s32[1,64]{1,0:T(1,128)}, u32[]{:S(2)}) copy-start(s32[1,64]{1,0:T(1,128)} %picks.1) | copy-start | bytes 772

commit v6 on v4

--- a/solution.py
+++ b/solution.py
@@ -115,8 +115,11 @@
     part[...] = total.astype(BF16).reshape(part.shape)
 
 
-def grads_kernel(core_ref, acts, got, gate, up, down, *rest):
-    sends, mine, sems = rest[:3], rest[3], rest[4]
+def grads_kernel(core_ref, acts, got_in, gate, up, down, *rest):
+    sends, (mine, got, sems) = rest[:3], rest[3:]
+    load = pltpu.make_async_copy(got_in, got, sems.at[3])
+    load.start()
+    load.wait()
     core = core_ref[0]
     rows = got.shape[0] * got.shape[2]
     stores = []
@@ -205,14 +208,18 @@
     grad = jax.ShapeDtypeStruct((2, units, width), BF16)
     results = pl.pallas_call(
         grads_kernel,
-        in_specs=[scalar, near, near],
+        in_specs=[scalar, near, far],
         out_specs=[far] * 3 + [near] * 3,
         out_shape=[grad] * 3 + [side] * 3,
-        scratch_shapes=[pltpu.VMEM((3, units, width), BF16), pltpu.SemaphoreType.DMA((3,))],
+        scratch_shapes=[
+            pltpu.VMEM((3, units, width), BF16),
+            pltpu.VMEM(got.shape, BF16),
+            pltpu.SemaphoreType.DMA((4,)),
+        ],
         cost_estimate=pl.CostEstimate(
             flops=12 * sources * units * width, bytes_accessed=6 * 2**20, transcendentals=0
         ),
-        compiler_params=medium,
+        compiler_params=pltpu.CompilerParams(vmem_limit_bytes=60000000),
     )(place, acts, got)
     theirs = [lax.all_gather(send, "core", axis=0) for send in results[3:]]
     filled, *grads = pl.pallas_call(

time: 124 us -> 123 us (level)
  Pallas kernels: 9.8 us -> 14.6 us
  blocking collectives: 66.1 us -> 63.5 us
  local copies, waits for them, and re-layouts: 4.58 us -> 2.36 us
    pallas_call x1, Pallas kernels: 1.87 us -> 5.71 us  [shards(): pl.pallas_call(grads_kernel, in_specs=[scalar, near, far], out_specs=[far...]
    all_to_all x1, blocking collectives: 24.1 us -> 21.1 us  [shards(): lax.all_to_all(summed.reshape(count, 2, width // 2), DEST, split_axis=0,...]
    unnamed x17 -> x15, local copies, waits for them, and re-layouts: 3.24 us -> 1.02 us
  transfers between devices with their start and end apart: 4 -> 4, of which waited for: 2 -> 2; matrix products, arithmetic and copies ran while one was open for 1% -> 1% of each run, Pallas kernels for 2% -> 5%
where the time goes in v6:
time: 123 us
  blocking collectives  63.5 us (52%)
  starting transfers between devices  26.2 us (21%)
  waiting for transfers between devices  14.9 us (12%)
  Pallas kernels  14.6 us (12%)
  local copies, waits for them, and re-layouts  2.36 us (2%)
    all_to_all x1, blocking collectives, shards(): lax.all_to_all(everyone, BATCH, split_axis=0, concat_axis=0, tiled=True)  32.7 us
    all_to_all x1, blocking collectives, shards(): lax.all_to_all(summed.reshape(count, 2, width // 2), DEST, split_axis=0,...  21.1 us
    all_to_all x1, starting transfers between devices, shards(): rows = lax.all_to_all(out, DEST, split_axis=0, concat_axis=0, tiled=True)  18.2 us
    all_to_all x1, waiting for transfers between devices, shards(): rows = lax.all_to_all(out, DEST, split_axis=0, concat_axis=0, tiled=True)  13.5 us
    all_gather x3, blocking collectives, shards(): theirs = [lax.all_gather(send, 'core', axis=0) for send in results[3:]]  9.71 us
    pallas_call x1, Pallas kernels, shards(): pl.pallas_call(grads_kernel, in_specs=[scalar, near, far], out_specs=[far...  5.71 us
    ppermute x2, starting transfers between devices, shards(): lax.ppermute(of(1 - core, *arrays), 'core', SWAP)  4.46 us
    pallas_call x1, Pallas kernels, shards(): pl.pallas_call(products_kernel, in_specs=[near] * 2, out_specs=[near] * 2...  4.44 us
  transfers between devices with their start and end apart: 4, of which 2 were waited for; matrix products, arithmetic and copies ran while one was open for 1% of the time, Pallas kernels for 5%

profile of v6, /device:TPU:1, one launch (start us, length us, event | category | flops | bytes accessed | tf_op | source)
XLA Modules:
  0.0 122.9 jit_solution(13407897058181854434)
XLA Ops:
  0.6 0.0 copy-start.4
  0.6 2.2 %shard_map.102 = bf16[64,16,128]{2,1,0:T(8,128)(2,1)} custom-call(s32[1,64]{1,0:T(1,128)} %picks.1, f32[1,64]{1,0:T(1,128)} %gates_in.1, bf16[128,1024]{1,0:T(8,128)(2,1)} %tokens_in.1, bf16[128,1024]{1,0:T(8,128)(2,1)} %cotangent_in.1), custom_call_target="tpu_custom_call" | custom-call | tf_op jit(solution)/shard_map/pallas_call | solution.py:167
  2.8 18.2 %all-to-all-start = ((bf16[64,16,128]{2,1,0:T(8,128)(2,1)}), bf16[64,16,128]{2,1,0:T(8,128)(2,1)S(1)}, u32[]{:S(2)}, u32[]{:S(2)}) async-start(bf16[64,16,128]{2,1,0:T(8,128)(2,1)} %shard_map.102), calls=%async_computation | async-start | bytes 524288 | tf_op jit(solution)/shard_map/all_to_all | solution.py:180
  21.0 0.0 copy-done.4
  21.0 1.2 constant_dynamic-slice_fusion.4
  22.2 0.0 copy-start.3
  22.2 0.1 pad_maximum_fusion.1
  22.3 2.4 %collective-permute-start = (bf16[2,176,1024]{2,1,0:T(8,128)(2,1)S(1)}, bf16[2,176,1024]{2,1,0:T(8,128)(2,1)S(1)}, u32[]{:S(2)}, u32[]{:S(2)}) collective-permute-start(bf16[2,176,1024]{2,1,0:T(8,128)(2,1)S(1)} %pad_maximum_fusion.1), channel_id=1, source_target_pairs={{0,32},{32,0},{1,33},{33,1},{2,34},{34,2},{3,35},{35,3},{4,36},{36... | collective-permute-start | bytes 2162696 | tf_op jit(solution)/shard_map/ppermute | solution.py:159
  24.7 0.0 copy-done.3
  24.7 0.1 constant_dynamic-slice_fusion.3
  24.8 2.1 %collective-permute-start.1 = (bf16[1,176,1024]{2,1,0:T(8,128)(2,1)S(1)}, bf16[1,176,1024]{2,1,0:T(8,128)(2,1)S(1)}, u32[]{:S(2)}, u32[]{:S(2)}) collective-permute-start(bf16[1,176,1024]{2,1,0:T(8,128)(2,1)S(1)} %get-tuple-element.33), channel_id=1, source_target_pairs={{0,32},{32,0},{1,33},{33,1},{2,34},{34,2},{3,35},{35,3},{4,36},{36... | collective-permute-start | bytes 1081352 | tf_op jit(solution)/shard_map/ppermute | solution.py:159
  26.9 0.1 maximum_bitcast_fusion
  27.0 1.4 %collective-permute-done.1 = bf16[1,176,1024]{2,1,0:T(8,128)(2,1)S(1)} collective-permute-done((bf16[1,176,1024]{2,1,0:T(8,128)(2,1)S(1)}, bf16[1,176,1024]{2,1,0:T(8,128)(2,1)S(1)}, u32[]{:S(2)}, u32[]{:S(2)}) %collective-permute-start.1) | collective-permute-done | bytes 360480 | tf_op jit(solution)/shard_map/ppermute | solution.py:159
  28.4 0.0 collective-permute-done
  28.4 0.1 maximum_bitcast_fusion.1
  28.5 0.2 pad_maximum_fusion.weights
  28.7 13.5 %all-to-all-done.rows = bf16[64,16,128]{2,1,0:T(8,128)(2,1)S(1)} async-done(((bf16[64,16,128]{2,1,0:T(8,128)(2,1)}), bf16[64,16,128]{2,1,0:T(8,128)(2,1)S(1)}, u32[]{:S(2)}, u32[]{:S(2)}) %all-to-all-start) | async-done | bytes 262176 | tf_op jit(solution)/shard_map/all_to_all | solution.py:180
  42.2 0.1 shard_map.103
  42.3 32.7 %all_to_all.20.got.got_in = bf16[8,2,64,1024]{3,2,1,0:T(8,128)(2,1)S(1)} all-to-all(bf16[8,2,64,1024]{3,2,1,0:T(8,128)(2,1)S(1)} %shard_map.103), channel_id=1, replica_groups=mesh['xh'=2,'y'=4,'core'=2,'xl'=2,'z'=16] {'xh','y'}, dimensions={0} | all-to-all | bytes 4194304 | tf_op jit(solution)/shard_map/all_to_all | solution.py:190
  75.0 0.0 copy-start
  75.0 4.4 %shard_map.104 = (bf16[8,64,1024]{2,1,0:T(8,128)(2,1)}, bf16[3,2,176,512]{3,2,1,0:T(8,128)(2,1)S(1)}) custom-call(bf16[8,2,64,1024]{3,2,1,0:T(8,128)(2,1)S(1)} %all_to_all.20.got.got_in, bf16[2,3,176,1024]{3,2,1,0:T(8,128)(2,1)S(1)} %pad_maximum_fusion.weights), custom_call_target="tpu_custom_call" | custom-call | flops 1845493760 | bytes 8388608 | tf_op jit(solution)/shard_map/pallas_call | solution.py:192
  79.4 0.0 copy-done
  79.4 0.0 copy-start.2
  79.4 1.0 copy-done.2
  80.4 3.6 %all-to-all-start.2 = ((bf16[8,64,1024]{2,1,0:T(8,128)(2,1)}), bf16[8,64,1024]{2,1,0:T(8,128)(2,1)S(1)}, u32[]{:S(2)}, u32[]{:S(2)}) async-start(bf16[8,64,1024]{2,1,0:T(8,128)(2,1)} %get-tuple-element.16), calls=%async_computation.2 | async-start | bytes 2097152 | tf_op jit(solution)/shard_map/all_to_all | solution.py:205
  84.0 5.7 %shard_map.105 = (bf16[2,176,1024]{2,1,0:T(8,128)(2,1)}, bf16[2,176,1024]{2,1,0:T(8,128)(2,1)}, bf16[2,176,1024]{2,1,0:T(8,128)(2,1)}, bf16[176,1024]{1,0:T(8,12...) custom-call(s32[1]{0:T(128)} %bitcast.2.core_ref, bf16[3,2,176,512]{3,2,1,0:T(8,128)(2,1)} %copy-done.2, ...), custom_call_target="tpu_custom_call" | custom-call | flops 1107296256 | bytes 6291456 | tf_op jit(solution)/shard_map/pallas_call | solution.py:209
  89.7 0.0 copy-start.6
  89.7 0.0 copy-start.5
  89.7 5.1 %all-gather = bf16[352,1024]{1,0:T(8,128)(2,1)S(1)} all-gather(bf16[176,1024]{1,0:T(8,128)(2,1)} %get-tuple-element.18), channel_id=2, replica_groups=mesh['xh'=2,'y'=4,'core'=2,'xl'=2,'z'=16] {'core'}, dimensions={0}, use_global_device_ids=true | all-gather | bytes 1081344 | tf_op jit(solution)/shard_map/all_gather | solution.py:224
  94.8 0.0 copy-done.6
  94.8 2.3 %all-gather.1 = bf16[352,1024]{1,0:T(8,128)(2,1)S(1)} all-gather(bf16[176,1024]{1,0:T(8,128)(2,1)S(1)} %copy-done.6), channel_id=3, replica_groups=mesh['xh'=2,'y'=4,'core'=2,'xl'=2,'z'=16] {'core'}, dimensions={0}, use_global_device_ids=true | all-gather | bytes 1081344 | tf_op jit(solution)/shard_map/all_gather | solution.py:224
  97.1 0.0 copy-done.5
  97.1 2.3 %all-gather.2 = bf16[352,1024]{1,0:T(8,128)(2,1)S(1)} all-gather(bf16[176,1024]{1,0:T(8,128)(2,1)S(1)} %copy-done.5), channel_id=4, replica_groups=mesh['xh'=2,'y'=4,'core'=2,'xl'=2,'z'=16] {'core'}, dimensions={0}, use_global_device_ids=true | all-gather | bytes 1081344 | tf_op jit(solution)/shard_map/all_gather | solution.py:224
  99.4 1.0 shard_map.106
  100.4 0.0 copy-start.1
  100.5 0.0 all-to-all-done.2.parts
  100.5 0.1 shard_map.107
  100.6 0.1 reshape.18
  100.7 21.1 %all_to_all.21 = bf16[64,2,512]{2,1,0:T(2,128)(2,1)S(1)} all-to-all(bf16[64,2,512]{2,1,0:T(2,128)(2,1)S(1)} %reshape.18), channel_id=1, replica_groups=mesh['xh'=2,'y'=4,'core'=2,'xl'=2,'z'=16] {'core','xl','z'}, dimensions={0} | all-to-all | bytes 262144 | tf_op jit(solution)/shard_map/all_to_all | solution.py:241
  121.8 0.0 copy-done.1
  121.8 1.0 shard_map.108
  (1 shorter events, 0.0 us)
Async XLA Ops:
  0.6 20.4 %copy-start.4 = (bf16[2,176,1024]{2,1,0:T(8,128)(2,1)S(1)}, bf16[2,176,1024]{2,1,0:T(8,128)(2,1)}, u32[]{:S(2)}) copy-start(bf16[2,176,1024]{2,1,0:T(8,128)(2,1)} %param.12) | copy-start | bytes 2162692
  2.8 39.4 %all-to-all-start = ((bf16[64,16,128]{2,1,0:T(8,128)(2,1)}), bf16[64,16,128]{2,1,0:T(8,128)(2,1)S(1)}, u32[]{:S(2)}, u32[]{:S(2)}) async-start(bf16[64,16,128]{2,1,0:T(8,128)(2,1)} %shard_map.102), calls=%async_computation | async-start | bytes 524288 | tf_op jit(solution)/shard_map/all_to_all | solution.py:180
  22.2 2.5 %copy-start.3 = (bf16[2,176,1024]{2,1,0:T(8,128)(2,1)S(1)}, bf16[2,176,1024]{2,1,0:T(8,128)(2,1)}, u32[]{:S(2)}) copy-start(bf16[2,176,1024]{2,1,0:T(8,128)(2,1)} %param.13) | copy-start | bytes 2162692
  22.3 6.1 %collective-permute-start = (bf16[2,176,1024]{2,1,0:T(8,128)(2,1)S(1)}, bf16[2,176,1024]{2,1,0:T(8,128)(2,1)S(1)}, u32[]{:S(2)}, u32[]{:S(2)}) collective-permute-start(bf16[2,176,1024]{2,1,0:T(8,128)(2,1)S(1)} %pad_maximum_fusion.1), channel_id=1, source_target_pairs={{0,32},{32,0},{1,33},{33,1},{2,34},{34,2},{3,35},{35,3},{4,36},{36... | collective-permute-start | bytes 2162696 | tf_op jit(solution)/shard_map/ppermute | solution.py:159
  24.8 3.6 %collective-permute-start.1 = (bf16[1,176,1024]{2,1,0:T(8,128)(2,1)S(1)}, bf16[1,176,1024]{2,1,0:T(8,128)(2,1)S(1)}, u32[]{:S(2)}, u32[]{:S(2)}) collective-permute-start(bf16[1,176,1024]{2,1,0:T(8,128)(2,1)S(1)} %get-tuple-element.33), channel_id=1, source_target_pairs={{0,32},{32,0},{1,33},{33,1},{2,34},{34,2},{3,35},{35,3},{4,36},{36... | collective-permute-start | bytes 1081352 | tf_op jit(solution)/shard_map/ppermute | solution.py:159
  75.0 4.4 %copy-start = (bf16[8,2,64,1024]{3,2,1,0:T(8,128)(2,1)}, bf16[8,2,64,1024]{3,2,1,0:T(8,128)(2,1)S(1)}, u32[]{:S(2)}) copy-start(bf16[8,2,64,1024]{3,2,1,0:T(8,128)(2,1)S(1)} %all_to_all.20.got.got_in) | copy-start | bytes 6291460
  79.4 1.0 copy-start.2
  80.4 20.0 %all-to-all-start.2 = ((bf16[8,64,1024]{2,1,0:T(8,128)(2,1)}), bf16[8,64,1024]{2,1,0:T(8,128)(2,1)S(1)}, u32[]{:S(2)}, u32[]{:S(2)}) async-start(bf16[8,64,1024]{2,1,0:T(8,128)(2,1)} %get-tuple-element.16), calls=%async_computation.2 | async-start | bytes 2097152 | tf_op jit(solution)/shard_map/all_to_all | solution.py:205
  89.7 5.1 %copy-start.6 = (bf16[176,1024]{1,0:T(8,128)(2,1)S(1)}, bf16[176,1024]{1,0:T(8,128)(2,1)}, u32[]{:S(2)}) copy-start(bf16[176,1024]{1,0:T(8,128)(2,1)} %get-tuple-element.19) | copy-start | bytes 1081348
  89.7 7.4 %copy-start.5 = (bf16[176,1024]{1,0:T(8,128)(2,1)S(1)}, bf16[176,1024]{1,0:T(8,128)(2,1)}, u32[]{:S(2)}) copy-start(bf16[176,1024]{1,0:T(8,128)(2,1)} %get-tuple-element.20) | copy-start | bytes 1081348
  100.4 21.4 %copy-start.1 = (s32[1,64]{1,0:T(1,128)S(1)}, s32[1,64]{1,0:T(1,128)}, u32[]{:S(2)}) copy-start(s32[1,64]{1,0:T(1,128)} %picks.1) | copy-start | bytes 772
